TPU v7x, 128 devices: a whole 4x4x4 slice. The times are simulated.
128 devices in a mesh: seq: 32 (over z, x, core), kvh: 4 (over y).
Axes of the slice: x: 4, y: 4, z: 4, core: 2. Of those that a mesh axis runs over, the one named last changes fastest.
Arguments:
- queries: bfloat16 [8192, 32, 128], P('seq', 'kvh'), may hold values from -6 to 6
- ctx_keys: bfloat16 [131072, 8, 128], P('seq', 'kvh'), may hold values from -6 to 6
- ctx_values: bfloat16 [131072, 8, 128], P('seq', 'kvh'), may hold values from -6 to 6
- new_keys: bfloat16 [8192, 8, 128], P('seq', 'kvh'), may hold values from -6 to 6
- new_values: bfloat16 [8192, 8, 128], P('seq', 'kvh'), may hold values from -6 to 6
- picks: int32 [8, 512, 2], P('kvh', 'seq'), may hold values from 0 to 31, all different within a row; in each aligned block of 16 rows (0 to 15, 16 to 31, ..., all dimensions but the last counted through in order) at most 2 rows name the same one
- out_weight: bfloat16 [4096, 4096], P('kvh'), may hold values from -0.09375 to 0.09375
Outputs:
- projected: bfloat16 [8192, 4096], P(('seq', 'kvh'))
Inputs may be any that keep to these rules, and one draw needn't show every extreme that they name: In each aligned block of 16 rows of picks (one key-value head's query blocks on one index of seq) the 2 entries of a row differ and no context block is named more than 2 times; some block is named exactly 2 times.
All inputs are finite; a program needn't handle non-finite values.
Results may differ from a plain program's by a relative error of at most 0.015.
Values may be sent and summed in bfloat16 or wider, within the bound.
A program may use at most 256 MiB of HBM per device.

v0:
```python
import math

import jax
import jax.numpy as jnp
from jax import lax
from jax.sharding import PartitionSpec as P

KB = 4096


NEGATIVE = -1e30


def attend(query_rows, key_rows, value_rows):
    score_scale = float(query_rows.shape[-1]) ** (-0.5)
    scores = jnp.dot(query_rows, key_rows.T, preferred_element_type=jnp.float32) * score_scale
    row_max = jnp.max(scores, axis=1, keepdims=True)
    exponent = jnp.exp(scores - row_max)
    row_total = jnp.sum(exponent, axis=1)
    numerator = jnp.dot(
        exponent.astype(jnp.bfloat16), value_rows, preferred_element_type=jnp.float32
    )
    return (numerator / row_total[:, None], row_max[:, 0] + jnp.log(row_total))


def attend_blocks(query_rows, key_rows, value_rows):
    row_count = query_rows.shape[0]
    feature = query_rows.shape[1]
    step_rows = math.gcd(row_count, 1024)

    def one_block(block_rows):
        return attend(block_rows, key_rows, value_rows)

    outputs, lse_rows = lax.map(
        one_block, query_rows.reshape(row_count // step_rows, step_rows, feature)
    )
    return (outputs.reshape(row_count, feature), lse_rows.reshape(row_count))


def absorb(state, piece, piece_start, own_queries, positions):
    key_rows, value_rows = piece
    piece_rows = key_rows.shape[0]
    columns = jnp.arange(piece_rows, dtype=jnp.int32)
    allowed = (columns[None, :] <= positions[:, None]) & (
        columns[None, :] // KB == positions[:, None] // KB
    )
    score_scale = float(own_queries.shape[-1]) ** (-0.5)

    def update(current):
        running_max, running_total, running_sum = current
        maxima = []
        totals = []
        numerators = []
        for head_index in range(key_rows.shape[1]):
            scores = (
                jnp.dot(
                    own_queries[head_index],
                    key_rows[:, head_index].T,
                    preferred_element_type=jnp.float32,
                )
                * score_scale
            )
            scores = jnp.where(allowed, scores, NEGATIVE)
            new_max = jnp.maximum(running_max[head_index], jnp.max(scores, axis=1))
            exponent = jnp.where(allowed, jnp.exp(scores - new_max[:, None]), 0.0)
            fade_factor = jnp.exp(running_max[head_index] - new_max)
            totals.append(running_total[head_index] * fade_factor + jnp.sum(exponent, axis=1))
            product = jnp.dot(
                exponent.astype(jnp.bfloat16),
                value_rows[:, head_index],
                preferred_element_type=jnp.float32,
            )
            numerators.append(running_sum[head_index] * fade_factor[:, None] + product)
            maxima.append(new_max)
        return (jnp.stack(maxima), jnp.stack(totals), jnp.stack(numerators))

    lowest = positions[0] // KB * KB
    touches = (piece_start + piece_rows > lowest) & (piece_start <= positions[-1])
    return lax.cond(touches, update, lambda current: current, state)


def take_slots(table, slot_ids):
    return table[slot_ids]


def on_device(queries, ctx_keys, ctx_values, new_keys, new_values, picks, out_weight):
    seq_count = lax.axis_size("seq")
    my_index = lax.axis_index("seq")
    rows_dev = queries.shape[0]
    local_heads = queries.shape[1]
    head_dim = queries.shape[2]
    kv_local = ctx_keys.shape[1]
    group_size = local_heads // kv_local
    own_queries = queries.reshape(rows_dev, kv_local, group_size, head_dim).transpose(1, 0, 2, 3)
    own_queries = own_queries.reshape(kv_local, rows_dev * group_size, head_dim)
    positions = (
        my_index * rows_dev + jnp.arange(rows_dev * group_size, dtype=jnp.int32) // group_size
    )
    start_state = (
        jnp.full((kv_local, rows_dev * group_size), NEGATIVE, jnp.float32),
        jnp.zeros((kv_local, rows_dev * group_size), jnp.float32),
        jnp.zeros((kv_local, rows_dev * group_size, head_dim), jnp.float32),
    )
    own_state = absorb(
        start_state,
        (
            lax.all_gather(new_keys, "seq", axis=0, tiled=True),
            lax.all_gather(new_values, "seq", axis=0, tiled=True),
        ),
        jnp.int32(0),
        own_queries,
        positions,
    )
    run_max, run_total, run_sum = own_state
    own_out = (
        (run_sum / run_total[..., None])
        .reshape(kv_local, rows_dev, group_size, head_dim)
        .transpose(1, 0, 2, 3)
    )
    own_lse = (
        (run_max + jnp.log(run_total)).reshape(kv_local, rows_dev, group_size).transpose(1, 0, 2)
    )
    blocks_dev = picks.shape[1]
    pick_count = picks.shape[2]
    block_rows = rows_dev // blocks_dev
    capacity = max(2, 4 * blocks_dev // seq_count)
    slot_total = seq_count * capacity
    targets = picks.reshape(kv_local, blocks_dev * pick_count)
    onehot = (targets[:, :, None] == jnp.arange(seq_count, dtype=jnp.int32)[None, None, :]).astype(
        jnp.int32
    )
    earlier_count = jnp.cumsum(onehot, axis=1) - onehot
    slot_index = jnp.sum(earlier_count * onehot, axis=2)
    slot_ids = (targets * capacity + slot_index).reshape(kv_local, blocks_dev, pick_count)
    placing = onehot[:, :, :, None] * (
        slot_index[:, :, None, None] == jnp.arange(capacity, dtype=jnp.int32)
    ).astype(jnp.int32)
    placing = placing.reshape(kv_local, blocks_dev, pick_count, slot_total)
    dispatch = jnp.sum(placing, axis=2).astype(jnp.bfloat16)
    shaped = queries.reshape(blocks_dev, block_rows, kv_local, group_size, head_dim)
    outgoing = jnp.einsum(
        "hqs,qrhgd->shrgd", dispatch, shaped, preferred_element_type=jnp.float32
    ).astype(jnp.bfloat16)
    outgoing = outgoing.reshape(seq_count, capacity, kv_local, block_rows * group_size, head_dim)
    arrived = lax.all_to_all(outgoing, "seq", split_axis=0, concat_axis=0, tiled=True)
    source_count = arrived.shape[0]
    item_count = arrived.shape[1]
    outputs = []
    lse_list = []
    for head_index in range(kv_local):
        part_out, part_lse = attend_blocks(
            arrived[:, :, head_index].reshape(-1, head_dim),
            ctx_keys[:, head_index],
            ctx_values[:, head_index],
        )
        outputs.append(part_out.reshape(source_count, item_count, -1, head_dim))
        lse_list.append(part_lse.reshape(source_count, item_count, -1))
    returned_out = lax.all_to_all(
        jnp.stack(outputs, axis=2), "seq", split_axis=0, concat_axis=0, tiled=True
    )
    returned_lse = lax.all_to_all(
        jnp.stack(lse_list, axis=2), "seq", split_axis=0, concat_axis=0, tiled=True
    )
    got_out = returned_out.reshape(
        slot_total, kv_local, block_rows * group_size, head_dim
    ).transpose(1, 0, 2, 3)
    got_lse = returned_lse.reshape(slot_total, kv_local, block_rows * group_size).transpose(1, 0, 2)
    part_outs = [own_out]
    part_lses = [own_lse]
    for pick_index in range(pick_count):
        chosen_slots = slot_ids[:, :, pick_index]
        pick_out = jax.vmap(take_slots)(got_out, chosen_slots)
        pick_out = pick_out.reshape(
            kv_local, blocks_dev, block_rows, group_size, head_dim
        ).transpose(1, 2, 0, 3, 4)
        part_outs.append(pick_out.reshape(rows_dev, kv_local, group_size, head_dim))
        pick_lse = jax.vmap(take_slots)(got_lse, chosen_slots)
        pick_lse = pick_lse.reshape(kv_local, blocks_dev, block_rows, group_size).transpose(
            1, 2, 0, 3
        )
        part_lses.append(pick_lse.reshape(rows_dev, kv_local, group_size))
    all_out = jnp.stack(part_outs, axis=3)
    all_lse = jnp.stack(part_lses, axis=3)
    best = jnp.max(all_lse, axis=3, keepdims=True)
    shares = jnp.exp(all_lse - best)
    merged = jnp.sum(shares[..., None] * all_out, axis=3) / jnp.sum(shares, axis=3)[..., None]
    merged = merged.reshape(rows_dev, local_heads * head_dim).astype(jnp.bfloat16)
    return lax.psum_scatter(
        jnp.dot(merged, out_weight, preferred_element_type=jnp.float32).astype(jnp.bfloat16),
        "kvh",
        scatter_dimension=0,
        tiled=True,
    )


def solution(mesh):
    placed = (
        P("seq", "kvh", None),
        P("seq", "kvh", None),
        P("seq", "kvh", None),
        P("seq", "kvh", None),
        P("seq", "kvh", None),
        P("kvh", "seq", None),
        P("kvh", None),
    )
    return jax.shard_map(
        on_device, mesh=mesh, in_specs=placed, out_specs=P(("seq", "kvh"), None), check_vma=False
    )
```

profile of v0, /device:TPU:1, one launch (start us, length us, event | category | flops | bytes accessed | tf_op | source)
XLA Modules:
  0.0 532.7 jit_solution(11814409162067909121)
XLA Ops:
  16.6 9.5 %all-to-all-start = ((bf16[32,2,2,64,128]{4,1,3,2,0:T(2,128)(2,1)}), bf16[32,2,2,64,128]{4,1,3,2,0:T(2,128)(2,1)}, u32[]{:S(2)}, u32[]{:S(2)}) async-start(bf16[32,2,2,64,128]{4,1,3,2,0:T(2,128)(2,1)} %copy.96), calls=%async_computation | async-start | bytes 4194304 | tf_op jit(solution)/shard_map/all_to_all | solution.py:145
  41.9 12.6 %all-to-all-done = bf16[32,2,2,64,128]{4,1,3,2,0:T(2,128)(2,1)} async-done(((bf16[32,2,2,64,128]{4,1,3,2,0:T(2,128)(2,1)}), bf16[32,2,2,64,128]{4,1,3,2,0:T(2,128)(2,1)}, u32[]{:S(2)}, u32[]{:S(2)}) %all-to-all-start) | async-done | bytes 2097184 | tf_op jit(solution)/shard_map/all_to_all | solution.py:145
  60.1 105.7 %while.24 = (s32[]{:T(128)}, f32[4,1024,128]{2,1,0:T(8,128)}, f32[4,1024]{1,0:T(4,128)S(1)}, bf16[4,1024,128]{2,1,0:T(8,128)(2,1)S(1)}, bf16[4096,128]{1,0:T(8,1...) while((s32[]{:T(128)}, f32[4,1024,128]{2,1,0:T(8,128)}, f32[4,1024]{1,0:T(4,128)S(1)}, ...), condition=%wide.region_12.13_spmd, body=%wide.region_9.12_spmd.sunk | while | flops 2181168128 | bytes 53256796 | solution.py:34
  68.4 8.6 %fusion.134 = f32[1024]{0:T(1024)S(1)} fusion(f32[1024,4096]{1,0:T(8,128)} %get-tuple-element.467, f32[1024]{0:T(1024)S(1)} %get-tuple-element.468), kind=kLoop, calls=%fused_computation.6.clone.1 | loop fusion | flops 12581888 | bytes 16785408 | tf_op jit(solution)/shard_map/while/body/eval_jaxpr/reduce_sum | solution.py:19
  77.2 9.6 %fusion.135 = f32[4,1024,128]{2,1,0:T(8,128)} fusion(f32[4,1024,128]{2,1,0:T(8,128)} %get-tuple-element.510, s32[]{:T(128)} %get-tuple-element.509, bf16[4096,128]{1,0:T(8,128)(2,1)} %get-tuple-element.522, f32[1024,4096]{1,0:T(8,128)} %get-tuple-element.467, f32[1024]{0:T(1024)S(1)} %get-tuple-element.468, f32[1024]{0:T(1024)S(1)} %fusion.134), kind=kOutput, calls=%fused_computation.11.clone.1 | convolution fusion | flops 1086455808 | bytes 18358784 | tf_op jit(solution)/shard_map/while/body/eval_jaxpr/dot_general | solution.py:20
  94.8 8.6 %fusion.134 = f32[1024]{0:T(1024)S(1)} fusion(f32[1024,4096]{1,0:T(8,128)} %get-tuple-element.467, f32[1024]{0:T(1024)S(1)} %get-tuple-element.468), kind=kLoop, calls=%fused_computation.6.clone.1 | loop fusion | flops 12581888 | bytes 16785408 | tf_op jit(solution)/shard_map/while/body/eval_jaxpr/reduce_sum | solution.py:19
  103.5 9.7 %fusion.135 = f32[4,1024,128]{2,1,0:T(8,128)} fusion(f32[4,1024,128]{2,1,0:T(8,128)} %get-tuple-element.510, s32[]{:T(128)} %get-tuple-element.509, bf16[4096,128]{1,0:T(8,128)(2,1)} %get-tuple-element.522, f32[1024,4096]{1,0:T(8,128)} %get-tuple-element.467, f32[1024]{0:T(1024)S(1)} %get-tuple-element.468, f32[1024]{0:T(1024)S(1)} %fusion.134), kind=kOutput, calls=%fused_computation.11.clone.1 | convolution fusion | flops 1086455808 | bytes 18358784 | tf_op jit(solution)/shard_map/while/body/eval_jaxpr/dot_general | solution.py:20
  130.0 9.5 %fusion.135 = f32[4,1024,128]{2,1,0:T(8,128)} fusion(f32[4,1024,128]{2,1,0:T(8,128)} %get-tuple-element.510, s32[]{:T(128)} %get-tuple-element.509, bf16[4096,128]{1,0:T(8,128)(2,1)} %get-tuple-element.522, f32[1024,4096]{1,0:T(8,128)} %get-tuple-element.467, f32[1024]{0:T(1024)S(1)} %get-tuple-element.468, f32[1024]{0:T(1024)S(1)} %fusion.134), kind=kOutput, calls=%fused_computation.11.clone.1 | convolution fusion | flops 1086455808 | bytes 18358784 | tf_op jit(solution)/shard_map/while/body/eval_jaxpr/dot_general | solution.py:20
  156.3 9.5 %fusion.135 = f32[4,1024,128]{2,1,0:T(8,128)} fusion(f32[4,1024,128]{2,1,0:T(8,128)} %get-tuple-element.510, s32[]{:T(128)} %get-tuple-element.509, bf16[4096,128]{1,0:T(8,128)(2,1)} %get-tuple-element.522, f32[1024,4096]{1,0:T(8,128)} %get-tuple-element.467, f32[1024]{0:T(1024)S(1)} %get-tuple-element.468, f32[1024]{0:T(1024)S(1)} %fusion.134), kind=kOutput, calls=%fused_computation.11.clone.1 | convolution fusion | flops 1086455808 | bytes 18358784 | tf_op jit(solution)/shard_map/while/body/eval_jaxpr/dot_general | solution.py:20
  168.4 101.8 %while.25 = (s32[]{:T(128)}, f32[4,1024,128]{2,1,0:T(8,128)S(1)}, f32[4,1024]{1,0:T(4,128)S(1)}, bf16[4,1024,128]{2,1,0:T(8,128)(2,1)}, bf16[4096,128]{1,0:T(8,1...) while((s32[]{:T(128)}, f32[4,1024,128]{2,1,0:T(8,128)S(1)}, f32[4,1024]{1,0:T(4,128)S(1)}, ...), condition=%wide.region_16.17_spmd, body=%wide.region_13.16_spmd.sunk | while | flops 2181168128 | bytes 53256796 | solution.py:34
  168.6 9.0 %multiply_reduce_fusion.5 = (f32[1024]{0:T(1024)S(1)}, f32[1024,4096]{1,0:T(8,128)}) fusion(bf16[4096,128]{1,0:T(8,128)(2,1)S(1)} %get-tuple-element.497, bf16[4,1024,128]{2,1,0:T(8,128)(2,1)} %get-tuple-element.496, s32[]{:T(128)} %get-tuple-element.485), kind=kOutput, calls=%fused_computation.19.clone.1 | convolution fusion | flops 1082129408 | bytes 18092544 | tf_op jit(solution)/shard_map/while/body/eval_jaxpr/dot_general | solution.py:16
  177.6 8.6 %fusion.139 = f32[1024]{0:T(1024)S(1)} fusion(f32[1024,4096]{1,0:T(8,128)} %get-tuple-element.475, f32[1024]{0:T(1024)S(1)} %get-tuple-element.476), kind=kLoop, calls=%fused_computation.20.clone.1 | loop fusion | flops 12581888 | bytes 16785408 | tf_op jit(solution)/shard_map/while/body/eval_jaxpr/reduce_sum | solution.py:19
  194.0 9.0 %multiply_reduce_fusion.5 = (f32[1024]{0:T(1024)S(1)}, f32[1024,4096]{1,0:T(8,128)}) fusion(bf16[4096,128]{1,0:T(8,128)(2,1)S(1)} %get-tuple-element.497, bf16[4,1024,128]{2,1,0:T(8,128)(2,1)} %get-tuple-element.496, s32[]{:T(128)} %get-tuple-element.485), kind=kOutput, calls=%fused_computation.19.clone.1 | convolution fusion | flops 1082129408 | bytes 18092544 | tf_op jit(solution)/shard_map/while/body/eval_jaxpr/dot_general | solution.py:16
  219.4 9.0 %multiply_reduce_fusion.5 = (f32[1024]{0:T(1024)S(1)}, f32[1024,4096]{1,0:T(8,128)}) fusion(bf16[4096,128]{1,0:T(8,128)(2,1)S(1)} %get-tuple-element.497, bf16[4,1024,128]{2,1,0:T(8,128)(2,1)} %get-tuple-element.496, s32[]{:T(128)} %get-tuple-element.485), kind=kOutput, calls=%fused_computation.19.clone.1 | convolution fusion | flops 1082129408 | bytes 18092544 | tf_op jit(solution)/shard_map/while/body/eval_jaxpr/dot_general | solution.py:16
  244.8 9.0 %multiply_reduce_fusion.5 = (f32[1024]{0:T(1024)S(1)}, f32[1024,4096]{1,0:T(8,128)}) fusion(bf16[4096,128]{1,0:T(8,128)(2,1)S(1)} %get-tuple-element.497, bf16[4,1024,128]{2,1,0:T(8,128)(2,1)} %get-tuple-element.496, s32[]{:T(128)} %get-tuple-element.485), kind=kOutput, calls=%fused_computation.19.clone.1 | convolution fusion | flops 1082129408 | bytes 18092544 | tf_op jit(solution)/shard_map/while/body/eval_jaxpr/dot_general | solution.py:16
  300.0 39.5 %all-to-all-done.2 = f32[32,2,2,64,128]{4,3,1,2,0:T(8,128)} async-done(((f32[32,2,2,64,128]{4,3,1,2,0:T(8,128)}), f32[32,2,2,64,128]{4,3,1,2,0:T(8,128)}, u32[]{:S(2)}, u32[]{:S(2)}) %all-to-all-start.2) | async-done | bytes 4194336 | tf_op jit(solution)/shard_map/all_to_all | solution.py:158
  349.9 11.1 %le.29 = s32[1024,8192]{1,0:T(8,128)} iota(), iota_dimension=1 | iota | bytes 33554432 | tf_op jit(solution)/shard_map/le | solution.py:44
  361.1 118.5 %conditional.1 = (f32[2,1024]{1,0:T(2,128)S(1)}, f32[2,1024]{1,0:T(2,128)S(1)}, f32[2,1024,128]{2,1,0:T(8,128)S(1)}, f32[2,1024]{1,0:T(2,128)S(1)}) conditional(s32[]{:T(128)} %convert_element_type.50, () %tuple.25, (s32[]{:T(128)}, s32[1024,8192]{1,0:T(8,128)}, s32[1,8192]{1,0:T(1,128)S(1)}, s32[1024,1]{0,1:T(1,128)S(1)}, ...), branch_computations={%region_0.1_spmd, %region_1.6_spmd.clone.clone} | conditional | flops 8833829888 | bytes 366747744 | solution.py:79
  362.8 15.1 %fusion.48 = f32[1024,8192]{1,0:T(8,128)} fusion(bf16[1024,128]{1,0:T(8,128)(2,1)S(1)} %bitcast.193, bf16[8192,2,128]{2,0,1:T(8,128)(2,1)} %get-tuple-element.307), kind=kOutput, calls=%fused_computation.47 | convolution fusion | flops 2147483648 | bytes 35913728 | tf_op jit(solution)/shard_map/cond/branch_1_fun/dot_general | solution.py:56
  378.0 36.1 %fusion.36 = (f32[1024]{0:T(1024)S(1)}, f32[1024]{0:T(1024)S(1)}, pred[1024,8192]{1,0:T(32,128)(4,1)}, f32[1024,8192]{1,0:T(8,128)}) fusion(f32[1024,8192]{1,0:T(8,128)} %fusion.48, s32[1024]{0:T(1024)S(1)} %bitcast.211, s32[8192]{0:T(1024)S(1)} %bitcast.206, s32[1024,8192]{1,0:T(8,128)} %get-tuple-element.301, s32[1024]{0:T(1024)S(1)} %bitcast.212, ...), kind=kOutput, calls=%fused_computation.37 | convolution fusion | flops 2222979072 | bytes 111460352 | tf_op jit(solution)/shard_map/cond/branch_1_fun/dot_general | solution.py:56
  414.1 22.7 %fusion.71 = f32[1,1024,128]{2,1,0:T(8,128)S(1)} fusion(bf16[8192,2,128]{2,0,1:T(8,128)(2,1)} %get-tuple-element.308, pred[1024,8192]{1,0:T(32,128)(4,1)} %get-tuple-element.365, f32[1024,8192]{1,0:T(8,128)} %get-tuple-element.380, f32[1024]{0:T(1024)S(1)} %get-tuple-element.381, f32[1024]{0:T(1024)S(1)} %get-tuple-element.382), kind=kOutput, calls=%fused_computation.58 | convolution fusion | flops 2189557760 | bytes 44572672 | tf_op jit(solution)/shard_map/cond/branch_1_fun/dot_general | solution.py:68
  436.8 15.2 %fusion.66 = f32[1,1024,128]{2,1,0:T(8,128)S(1)} fusion(bf16[8192,2,128]{2,0,1:T(8,128)(2,1)S(1)} %copy-done.8, pred[1024,8192]{1,0:T(32,128)(4,1)S(1)} %copy-done, f32[1024,8192]{1,0:T(8,128)} %fusion.48, f32[1024]{0:T(1024)S(1)} %get-tuple-element.379, f32[1024]{0:T(1024)S(1)} %get-tuple-element.378), kind=kOutput, calls=%fused_computation.57 | convolution fusion | flops 2189557760 | bytes 44572672 | tf_op jit(solution)/shard_map/cond/branch_1_fun/dot_general | solution.py:68
  452.1 27.2 %fusion.39 = (f32[1024]{0:T(1024)S(1)}, f32[1024]{0:T(1024)S(1)}) fusion(pred[1024,8192]{1,0:T(32,128)(4,1)S(1)} %copy-done, f32[1024,8192]{1,0:T(8,128)} %get-tuple-element.380, f32[1024]{0:T(1024)S(1)} %get-tuple-element.381, f32[1024]{0:T(1024)S(1)} %get-tuple-element.379, f32[1024,8192]{1,0:T(8,128)} %fusion.48), kind=kLoop, calls=%fused_computation.40 | loop fusion | flops 83884032 | bytes 75513856 | tf_op jit(solution)/shard_map/cond/branch_1_fun/reduce_sum | solution.py:67
  496.4 29.5 %reduce-scatter.2.cloned.1.call-done = bf16[64,4096]{1,0:T(8,128)(2,1)} async-done(((bf16[256,4096]{1,0:T(8,128)(2,1)}), bf16[64,4096]{1,0:T(8,128)(2,1)}) %reduce-scatter.2.cloned.1.call-update) | async-done | bytes 524304 | tf_op jit(solution)/shard_map/reduce_scatter | solution.py:188
  (143 shorter events, 196.2 us)
Async XLA Ops:
  6.5 19.8 %copy-start.4 = (bf16[256,2,128]{2,1,0:T(2,128)(2,1)S(1)}, bf16[256,2,128]{2,1,0:T(2,128)(2,1)}, u32[]{:S(2)}) copy-start(bf16[256,2,128]{2,1,0:T(2,128)(2,1)} %param.17) | copy-start | bytes 393220
  6.5 20.5 %copy-start.1 = (bf16[4096,2,128]{2,1,0:T(2,128)(2,1)S(1)}, bf16[4096,2,128]{2,1,0:T(2,128)(2,1)}, u32[]{:S(2)}) copy-start(bf16[4096,2,128]{2,1,0:T(2,128)(2,1)} %param.14) | copy-start | bytes 6291460
  6.5 343.3 %all-gather.3.cloned.1.call-start = ((), (), s32[]{:S(2)}) async-start(), calls=%async_computation.4 | async-start | bytes 4325376 | tf_op jit(solution)/shard_map/all_gather | solution.py:107
  9.5 0.6 copy-start.5
  16.6 37.9 %all-to-all-start = ((bf16[32,2,2,64,128]{4,1,3,2,0:T(2,128)(2,1)}), bf16[32,2,2,64,128]{4,1,3,2,0:T(2,128)(2,1)}, u32[]{:S(2)}, u32[]{:S(2)}) async-start(bf16[32,2,2,64,128]{4,1,3,2,0:T(2,128)(2,1)} %copy.96), calls=%async_computation | async-start | bytes 4194304 | tf_op jit(solution)/shard_map/all_to_all | solution.py:145
  26.1 323.8 %all-gather.5.cloned.1.call-start = ((), (), s32[]{:S(2)}) async-start(), calls=%async_computation.5 | async-start | bytes 4325376 | tf_op jit(solution)/shard_map/all_gather | solution.py:108
  27.0 4.3 copy-start.2
  271.2 13.1 %all-to-all-start.1 = ((f32[32,1,256]{2,1,0:T(1,128)}), f32[32,1,256]{2,1,0:T(1,128)S(1)}, u32[]{:S(2)}, u32[]{:S(2)}) async-start(f32[32,1,256]{2,1,0:T(1,128)} %reshape.371), calls=%async_computation.1 | async-start | bytes 65536 | tf_op jit(solution)/shard_map/all_to_all | solution.py:161
  276.9 14.8 %copy-start.3 = (bf16[256,8,128]{2,1,0:T(8,128)(2,1)S(1)}, bf16[256,8,128]{2,1,0:T(8,128)(2,1)}, u32[]{:S(2)}) copy-start(bf16[256,8,128]{2,1,0:T(8,128)(2,1)} %param.13) | copy-start | bytes 1572868
  276.9 15.7 %copy-start.6 = (s32[2,32]{1,0:T(2,128)S(1)}, s32[2,32]{1,0:T(2,128)}, u32[]{:S(2)}) copy-start(s32[2,32]{1,0:T(2,128)} %copy-done.5) | copy-start | bytes 772
  276.9 17.2 %copy-start.7 = (s32[2,16,2]{1,2,0:T(2,128)S(1)}, s32[2,16,2]{1,2,0:T(2,128)}, u32[]{:S(2)}) copy-start(s32[2,16,2]{1,2,0:T(2,128)} %param.18) | copy-start | bytes 772
  284.3 55.2 %all-to-all-start.2 = ((f32[32,2,2,64,128]{4,3,1,2,0:T(8,128)}), f32[32,2,2,64,128]{4,3,1,2,0:T(8,128)}, u32[]{:S(2)}, u32[]{:S(2)}) async-start(f32[32,2,2,64,128]{4,3,1,2,0:T(8,128)} %pad_maximum_fusion.3), calls=%async_computation.2 | async-start | bytes 8388608 | tf_op jit(solution)/shard_map/all_to_all | solution.py:158
  289.1 236.8 %reduce-scatter.2.cloned.1.call-start = ((), (), s32[]{:S(2)}) async-start(), calls=%async_computation.6 | async-start | bytes 2621440 | tf_op jit(solution)/shard_map/reduce_scatter | solution.py:188
  414.1 22.7 %copy-start = (pred[1024,8192]{1,0:T(32,128)(4,1)S(1)}, pred[1024,8192]{1,0:T(32,128)(4,1)}, u32[]{:S(2)}) copy-start(pred[1024,8192]{1,0:T(32,128)(4,1)} %get-tuple-element.365) | copy-start | bytes 25165828 | tf_op jit(solution)/shard_map/cond
  414.1 22.7 %copy-start.8 = (bf16[8192,2,128]{2,0,1:T(8,128)(2,1)S(1)}, bf16[8192,2,128]{2,0,1:T(8,128)(2,1)}, u32[]{:S(2)}) copy-start(bf16[8192,2,128]{2,0,1:T(8,128)(2,1)} %get-tuple-element.308) | copy-start | bytes 12582916 | tf_op jit(solution)/shard_map/cond
Sparse Core Ops, SparseCore 0:
  9.7 61.7 all-gather.2
  73.8 45.6 all-gather.4
  496.5 29.3 reduce-scatter.1
where the time goes:
time: 538 us; the launch traced here: 533 us
  matrix products  235 us (44%)
  other arithmetic  109 us (20%)
  waiting for transfers between devices  85 us (16%)
  local copies, waits for them, and re-layouts  65.5 us (12%)
  starting transfers between devices  20.3 us (4%)
  between operations  17 us (3%)
    reduce_sum x8, other arithmetic, attend(): row_total = jnp.sum(exponent, axis=1)  69 us
    dot_general x8, matrix products, attend(): jnp.dot(exponent.astype(jnp.bfloat16), value_rows, preferred_element_type...  68.9 us
    dot_general x8, matrix products, attend(): jnp.dot(query_rows, key_rows.T, preferred_element_type=jnp.float32)  68.5 us
    dot_general x2, matrix products, update(): jnp.dot(own_queries[head_index], key_rows[:, head_index].T, preferred_ele...  51.1 us
    all_to_all x1, waiting for transfers between devices, on_device(): lax.all_to_all(jnp.stack(outputs, axis=2), 'seq', split_axis=0, concat_ax...  39.5 us
    dot_general x2, matrix products, update(): jnp.dot(exponent.astype(jnp.bfloat16), value_rows[:, head_index], preferr...  37.9 us
    reduce_scatter x1, waiting for transfers between devices, on_device(): lax.psum_scatter(jnp.dot(merged, out_weight, preferred_element_type=jnp.f...  29.5 us
    reduce_sum x1, other arithmetic, update(): jnp.sum(exponent, axis=1)  27.2 us
  transfers between devices with their start and end apart: 6, of which 4 were waited for; matrix products, arithmetic and copies ran while one was open for 49% of the time, Pallas kernels for 0%

commit v1 on v0

v1 whole, which is shorter than its diff:
```python
import functools

import jax
import jax.numpy as jnp
from jax import lax
from jax.experimental import pallas as pl
from jax.experimental.pallas import tpu as pltpu
from jax.sharding import PartitionSpec as P

LOG2E = 1.4426950408889634
NT = (((1,), (1,)), ((), ()))
TN = (((0,), (0,)), ((), ()))
VM = pl.BlockSpec(memory_space=pltpu.VMEM)
SM = pl.BlockSpec(memory_space=pltpu.SMEM)
KB = 4096
BIG = 60 * 2**20
EXTRA = 16


def split_queries(rows):
    scale = LOG2E * float(rows.shape[-1]) ** -0.5
    scaled = rows.astype(jnp.float32) * scale
    high = scaled.astype(jnp.bfloat16)
    low = (scaled - high.astype(jnp.float32)).astype(jnp.bfloat16)
    return jnp.concatenate([high, low], axis=1)


def scores_of(keys, split):
    return lax.dot_general(
        jnp.concatenate([keys, keys], axis=1), split, NT, preferred_element_type=jnp.float32
    )


def attend_tile(rows, keys_at, values_t_at, chunks):
    split = split_queries(rows)
    top = total = acc = None
    now = scores_of(keys_at(0), split)
    for c in range(chunks):
        later = scores_of(keys_at(c + 1), split) if c + 1 < chunks else None
        best = jnp.max(now, axis=0, keepdims=True)
        best = best if top is None else jnp.maximum(top, best)
        e = jnp.exp2(now - best)
        part = jnp.sum(e, axis=0, keepdims=True)
        out = jnp.dot(values_t_at(c), e.astype(jnp.bfloat16), preferred_element_type=jnp.float32)
        if top is None:
            acc, total = out, part
        else:
            fade = jnp.exp2(top - best)
            acc, total = acc * fade + out, total * fade + part
        top, now = best, later
    return acc / total, top + jnp.log2(total)


def three_parts(row):
    high = row.astype(jnp.bfloat16).astype(jnp.float32)
    rest = row - high
    mid = rest.astype(jnp.bfloat16).astype(jnp.float32)
    fill = jnp.zeros((EXTRA - 3, row.shape[1]), jnp.float32)
    return jnp.concatenate([high, mid, rest - mid, fill], axis=0).astype(jnp.bfloat16)


def place_kernel(picks_ref, q_ref, out_ref, slot_ref, count_ref):
    heads, blocks, picked = picks_ref.shape
    item = q_ref.shape[1] // blocks
    owners = out_ref.shape[0]
    out_ref[...] = jnp.zeros_like(out_ref)

    def clear(i, _):
        for h in range(heads):
            count_ref[h, i] = 0
        return 0

    lax.fori_loop(0, owners, clear, 0)
    for h in range(heads):

        def one(q, _):
            rows = q_ref[h, pl.ds(pl.multiple_of(q * item, item), item), :]
            for p in range(picked):
                t = picks_ref[h, q, p]
                c = count_ref[h, t]
                count_ref[h, t] = c + 1
                slot_ref[h, q, p] = c
                out_ref[t, h, pl.ds(pl.multiple_of(c * item, item), item), :] = rows
            return 0

        lax.fori_loop(0, blocks, one, 0)


def place(picks, q):
    heads, rows, feature = q.shape
    return pl.pallas_call(
        place_kernel,
        out_shape=(
            jax.ShapeDtypeStruct((32, heads, 128, feature), jnp.bfloat16),
            jax.ShapeDtypeStruct(picks.shape, jnp.int32),
        ),
        in_specs=[SM, VM],
        out_specs=(VM, SM),
        scratch_shapes=[pltpu.SMEM((heads, 32), jnp.int32)],
        compiler_params=pltpu.CompilerParams(vmem_limit_bytes=BIG),
    )(picks, q)


def context_kernel(q_ref, k_ref, v_ref, out_ref):
    sources, heads, slot_rows, feature = q_ref.shape
    group, step = 4, 1024

    def tile(i, _):
        first = i * group
        for h in range(heads):
            rows = jnp.concatenate([q_ref[first + j, h] for j in range(group)], axis=0)
            out, lse = attend_tile(
                rows,
                lambda c: k_ref[h, c * step : (c + 1) * step, :],
                lambda c: v_ref[h, :, c * step : (c + 1) * step],
                KB // step,
            )
            out = out.T.astype(jnp.bfloat16)
            for j in range(group):
                cut = slice(j * slot_rows, (j + 1) * slot_rows)
                out_ref[first + j, h, 0:slot_rows, :] = out[cut, :]
                out_ref[first + j, h, slot_rows : slot_rows + EXTRA, :] = three_parts(lse[:, cut])
        return 0

    lax.fori_loop(0, sources // group, tile, 0)


def context(arrived, keys, values_t):
    sources, heads, slot_rows, feature = arrived.shape
    return pl.pallas_call(
        context_kernel,
        out_shape=jax.ShapeDtypeStruct((sources, heads, slot_rows + EXTRA, feature), jnp.bfloat16),
        in_specs=[VM, VM, VM],
        out_specs=VM,
        compiler_params=pltpu.CompilerParams(vmem_limit_bytes=BIG),
    )(arrived, keys, values_t)


def own_kernel(picks_ref, slot_ref, q_ref, kv_ref, ret_ref, out_ref, acc_ref, top_ref, sum_ref):
    heads, rows, feature = q_ref.shape
    blocks, picked = picks_ref.shape[1:]
    item = rows // blocks
    block_rows = out_ref.shape[0] // blocks
    group = item // block_rows
    span = kv_ref.shape[3]
    mine = lax.rem(lax.axis_index("seq"), kv_ref.shape[0])

    def absorb(j, masked):
        for h in range(heads):
            split = split_queries(q_ref[h])
            s = scores_of(kv_ref[j, 0, h], split)
            if masked:
                key_at = lax.broadcasted_iota(jnp.int32, s.shape, 0)
                col = lax.broadcasted_iota(jnp.int32, s.shape, 1)
                row_at = (col // item) * block_rows + lax.rem(col, block_rows)
                s = jnp.where(key_at <= row_at, s, -1e30)
            best = jnp.max(s, axis=0, keepdims=True)
            if not masked:
                best = jnp.maximum(top_ref[h, 0:1, :], best)
            e = jnp.exp2(s - best)
            part = jnp.sum(e, axis=0, keepdims=True)
            o = lax.dot_general(
                kv_ref[j, 1, h], e.astype(jnp.bfloat16), TN, preferred_element_type=jnp.float32
            )
            if masked:
                acc_ref[h] = o
                sum_ref[h, 0:1, :] = part
            else:
                fade = jnp.exp2(top_ref[h, 0:1, :] - best)
                acc_ref[h] = acc_ref[h] * fade + o
                sum_ref[h, 0:1, :] = sum_ref[h, 0:1, :] * fade + part
            top_ref[h, 0:1, :] = best

    absorb(mine, True)

    def step(j, _):
        absorb(j, False)
        return 0

    lax.fori_loop(0, mine, step, 0)
    for h in range(heads):
        total = sum_ref[h, 0:1, :]
        own = (acc_ref[h] / total).T
        lses = [top_ref[h, 0:1, :] + jnp.log2(total)]
        for p in range(picked):
            pieces = []
            for q in range(blocks):
                t, c = picks_ref[h, q, p], slot_ref[h, q, p]
                lse = jnp.sum(
                    ret_ref[t, h, 2 * item : 2 * item + EXTRA, :].astype(jnp.float32),
                    axis=0,
                    keepdims=True,
                )
                pieces.append(jnp.where(c == 0, lse[:, 0:item], lse[:, item : 2 * item]))
            lses.append(jnp.concatenate(pieces, axis=1))
        best = functools.reduce(jnp.maximum, lses)
        shares = [jnp.exp2(x - best) for x in lses]
        whole = functools.reduce(jnp.add, shares)
        shares = [x / whole for x in shares]
        fill = [jnp.zeros_like(best)] * (8 - len(shares))
        columns = jnp.concatenate(shares + fill, axis=0).T
        for q in range(blocks):
            cut = slice(q * item, (q + 1) * item)
            mix = own[cut, :] * columns[cut, 0:1]
            for p in range(picked):
                t, c = picks_ref[h, q, p], slot_ref[h, q, p]
                got = ret_ref[t, h, pl.ds(pl.multiple_of(c * item, item), item), :]
                mix = mix + got.astype(jnp.float32) * columns[cut, p + 1 : p + 2]
            mix = mix.astype(jnp.bfloat16)
            for g in range(group):
                at = (h * group + g) * feature
                out_ref[q * block_rows : (q + 1) * block_rows, at : at + feature] = mix[
                    g * block_rows : (g + 1) * block_rows, :
                ]


def own_and_merge(picks, slots, q, kv, ret):
    heads, rows, feature = q.shape
    return pl.pallas_call(
        own_kernel,
        out_shape=jax.ShapeDtypeStruct((256, 8 * feature), jnp.bfloat16),
        in_specs=[SM, SM, VM, VM, VM],
        out_specs=VM,
        scratch_shapes=[
            pltpu.VMEM((heads, feature, rows), jnp.float32),
            pltpu.VMEM((heads, 8, rows), jnp.float32),
            pltpu.VMEM((heads, 8, rows), jnp.float32),
        ],
        compiler_params=pltpu.CompilerParams(vmem_limit_bytes=BIG),
    )(picks, slots, q, kv, ret)


def on_device(queries, ctx_keys, ctx_values, new_keys, new_values, picks, out_weight):
    q = queries.reshape(16, 16, 2, 4, 128).transpose(2, 0, 3, 1, 4).reshape(2, 1024, 128)
    outgoing, slots = place(picks, q)
    arrived = lax.all_to_all(outgoing, "seq", split_axis=0, concat_axis=0, tiled=True)
    keys = ctx_keys.transpose(1, 0, 2)
    values_t = ctx_values.transpose(1, 2, 0)
    kv = jnp.stack([new_keys.transpose(1, 0, 2), new_values.transpose(1, 0, 2)])
    groups = [list(range(16)), list(range(16, 32))]
    kv = lax.all_gather(kv, "seq", axis=0, axis_index_groups=groups)
    done = context(arrived, keys, values_t)
    ret = lax.all_to_all(done, "seq", split_axis=0, concat_axis=0, tiled=True)
    merged = own_and_merge(picks, slots, q, kv, ret)
    return lax.psum_scatter(
        jnp.dot(merged, out_weight, preferred_element_type=jnp.float32).astype(jnp.bfloat16),
        "kvh",
        scatter_dimension=0,
        tiled=True,
    )


def solution(mesh):
    placed = (
        P("seq", "kvh", None),
        P("seq", "kvh", None),
        P("seq", "kvh", None),
        P("seq", "kvh", None),
        P("seq", "kvh", None),
        P("kvh", "seq", None),
        P("kvh", None),
    )
    return jax.shard_map(
        on_device, mesh=mesh, in_specs=placed, out_specs=P(("seq", "kvh"), None), check_vma=False
    )
```

time: 538 us -> 219 us (0.41)
  matrix products: 235 us -> 7.24 us
  other arithmetic: 109 us -> 0.75 us
  Pallas kernels: 0 us -> 58.7 us
  local copies, waits for them, and re-layouts: 65.5 us -> 14.5 us
  blocking collectives: 0 us -> 39.8 us
  starting transfers between devices: 20.3 us -> 9.49 us
  waiting for transfers between devices: 85 us -> 74.3 us
    dot_general x21 -> x0, matrix products: 228 us -> none  [the longest x8 68.9 us: attend(): jnp.dot(exponent.astype(jnp.bfloat16), value_rows, preferred_element_type...]
    reduce_sum x13 -> x0, other arithmetic: 100 us -> none  [the longest x8 69 us: attend(): row_total = jnp.sum(exponent, axis=1)]
    pallas_call x0 -> x3, Pallas kernels: none -> 58.7 us  [the longest x1 46.5 us: context(): pl.pallas_call(context_kernel, out_shape=jax.ShapeDtypeStruct((sources, h...]
    all_to_all x2 -> x0, waiting for transfers between devices: 42.8 us -> none  [the longest x1 39.5 us: on_device(): lax.all_to_all(jnp.stack(outputs, axis=2), 'seq', split_axis=0, concat_ax...]
    all_to_all x0 -> x1, blocking collectives: none -> 39.8 us  [on_device(): ret = lax.all_to_all(done, 'seq', split_axis=0, concat_axis=0, tiled=True)]
    reduce_scatter x1, waiting for transfers between devices: 29.5 us -> 45.7 us  [on_device(): lax.psum_scatter(jnp.dot(merged, out_weight, preferred_element_type=jnp.f...]
    all_to_all x1, waiting for transfers between devices: 12.6 us -> 28.5 us  [on_device(): lax.all_to_all(outgoing, 'seq', split_axis=0, concat_axis=0, tiled=True)]
    slice x5 -> x0, local copies, waits for them, and re-layouts: 13.2 us -> none  [the longest x1 4.28 us: on_device(): ctx_keys[:, head_index]]
  transfers between devices with their start and end apart: 6 -> 3, of which waited for: 4 -> 2; matrix products, arithmetic and copies ran while one was open for 49% -> 6% of each run, Pallas kernels for 0% -> 23%
where the time goes in v1:
time: 219 us; the launch traced here: 218 us
  waiting for transfers between devices  74.3 us (34%)
  Pallas kernels  58.7 us (27%)
  blocking collectives  39.8 us (18%)
  local copies, waits for them, and re-layouts  14.5 us (7%)
  between operations  13.4 us (6%)
  starting transfers between devices  9.49 us (4%)
  matrix products  7.24 us (3%)
    pallas_call x1, Pallas kernels, context(): pl.pallas_call(context_kernel, out_shape=jax.ShapeDtypeStruct((sources, h...  46.5 us
    reduce_scatter x1, waiting for transfers between devices, on_device(): lax.psum_scatter(jnp.dot(merged, out_weight, preferred_element_type=jnp.f...  45.7 us
    all_to_all x1, blocking collectives, on_device(): ret = lax.all_to_all(done, 'seq', split_axis=0, concat_axis=0, tiled=True)  39.8 us
    all_to_all x1, waiting for transfers between devices, on_device(): lax.all_to_all(outgoing, 'seq', split_axis=0, concat_axis=0, tiled=True)  28.5 us
    unnamed x7, local copies, waits for them, and re-layouts  11.5 us
    all_to_all x1, starting transfers between devices, on_device(): lax.all_to_all(outgoing, 'seq', split_axis=0, concat_axis=0, tiled=True)  9.45 us
    pallas_call x1, Pallas kernels, own_and_merge(): pl.pallas_call(own_kernel, out_shape=jax.ShapeDtypeStruct((256, 8 * featu...  8.78 us
    dot_general x1, matrix products, on_device(): jnp.dot(merged, out_weight, preferred_element_type=jnp.float32)  7.24 us
  transfers between devices with their start and end apart: 3, of which 2 were waited for; matrix products, arithmetic and copies ran while one was open for 6% of the time, Pallas kernels for 23%

profile of v1, /device:TPU:1, one launch (start us, length us, event | category | flops | bytes accessed | tf_op | source)
XLA Modules:
  0.0 218.2 jit_solution(10644923444352149011)
XLA Ops:
  6.5 0.0 copy-start.1
  6.5 0.0 all-gather.3.cloned.1.call-start
  6.5 1.0 copy_bitcast_fusion.1
  7.6 0.7 pad_maximum_fusion
  8.3 0.0 all-gather.3.cloned.1.call-update
  8.3 2.0 copy.14
  10.3 0.0 copy-done.1
  10.3 0.7 copy.20.picks_ref
  11.0 3.5 %shard_map.73 = (bf16[32,2,128,128]{3,2,1,0:T(8,128)(2,1)}, s32[2,16,2]{2,1,0:T(8,128)}) custom-call(s32[2,16,2]{2,1,0:T(8,128)} %copy.20.picks_ref, bf16[2,1024,128]{2,1,0:T(8,128)(2,1)} %bitcast.21), custom_call_target="tpu_custom_call" | custom-call | tf_op jit(solution)/shard_map/pallas_call | solution.py:91
  14.5 9.4 %all-to-all-start = ((bf16[32,2,128,128]{3,2,1,0:T(8,128)(2,1)}), bf16[32,2,128,128]{3,2,1,0:T(8,128)(2,1)S(1)}, u32[]{:S(2)}, u32[]{:S(2)}) async-start(bf16[32,2,128,128]{3,2,1,0:T(8,128)(2,1)} %get-tuple-element.8), calls=%async_computation | async-start | bytes 4194304 | tf_op jit(solution)/shard_map/all_to_all | solution.py:236
  23.9 0.0 reduce-scatter.2.cloned.1.call-start
  24.0 3.2 %copy.24 = bf16[4096,2,128]{2,0,1:T(8,128)(2,1)} copy(bf16[4096,2,128]{2,1,0:T(2,128)(2,1)} %param.8) | data formatting | bytes 4194304 | tf_op args[1]
  27.2 6.2 %copy.19 = bf16[4096,2,128]{0,2,1:T(8,128)(2,1)} copy(bf16[4096,2,128]{2,1,0:T(2,128)(2,1)} %param.9) | data formatting | bytes 4194304 | tf_op args[2]
  33.4 28.5 %all-to-all-done.q_ref = bf16[32,2,128,128]{3,2,1,0:T(8,128)(2,1)S(1)} async-done(((bf16[32,2,128,128]{3,2,1,0:T(8,128)(2,1)}), bf16[32,2,128,128]{3,2,1,0:T(8,128)(2,1)S(1)}, u32[]{:S(2)}, u32[]{:S(2)}) %all-to-all-start) | async-done | bytes 2097184 | tf_op jit(solution)/shard_map/all_to_all | solution.py:236
  61.9 0.0 copy-start
  61.9 1.4 copy-done
  63.3 46.5 %shard_map.74 = bf16[32,2,144,128]{3,2,1,0:T(8,128)(2,1)} custom-call(bf16[32,2,128,128]{3,2,1,0:T(8,128)(2,1)} %copy-done, bf16[2,4096,128]{2,1,0:T(8,128)(2,1)} %bitcast.19, bf16[2,128,4096]{2,1,0:T(8,128)(2,1)} %bitcast.20), custom_call_target="tpu_custom_call" | custom-call | tf_op jit(solution)/shard_map/pallas_call | solution.py:130
  109.8 39.8 %all_to_all.10.ret_ref = bf16[32,2,144,128]{3,2,1,0:T(8,128)(2,1)} all-to-all(bf16[32,2,144,128]{3,2,1,0:T(8,128)(2,1)} %shard_map.74), channel_id=1, replica_groups=mesh['seq'=32,'kvh'=4] {'seq'}, dimensions={0} | all-to-all | bytes 4718592 | tf_op jit(solution)/shard_map/all_to_all | solution.py:243
  149.5 0.0 all-gather.3.cloned.1.call-done
  149.5 8.8 %shard_map.75 = bf16[256,1024]{1,0:T(8,128)(2,1)} custom-call(s32[2,16,2]{2,1,0:T(8,128)} %copy.20.picks_ref, s32[2,16,2]{2,1,0:T(8,128)} %get-tuple-element.7.slot_ref, bf16[2,1024,128]{2,1,0:T(8,128)(2,1)} %bitcast.22, bf16[16,2,2,256,128]{4,3,2,1,0:T(8,128)(2,1)} %bitcast.23, bf16[32,2,144,128]{3,2,1,0:T(8,128)(2,1)} %all_to_all.10.ret_ref), custom_call_target="tpu_custom_call" | custom-call | tf_op jit(solution)/shard_map/pallas_call | solution.py:219
  158.3 7.2 %convolution_convert_fusion = bf16[256,4096]{1,0:T(8,128)(2,1)} fusion(bf16[256,1024]{1,0:T(8,128)(2,1)} %shard_map.75, bf16[1024,4096]{1,0:T(8,128)(2,1)} %param.13), kind=kOutput, calls=%fused_computation | convolution fusion | flops 2148532224 | bytes 11010048 | tf_op jit(solution)/shard_map/dot_general | solution.py:246
  165.6 0.0 reduce-scatter.2.cloned.1.call-update
  165.6 45.7 %reduce-scatter.2.cloned.1.call-done = bf16[64,4096]{1,0:T(8,128)(2,1)} async-done(((bf16[256,4096]{1,0:T(8,128)(2,1)}), bf16[64,4096]{1,0:T(8,128)(2,1)}) %reduce-scatter.2.cloned.1.call-update) | async-done | bytes 524304 | tf_op jit(solution)/shard_map/reduce_scatter | solution.py:245
Async XLA Ops:
  6.5 3.8 %copy-start.1 = (s32[2,16,2]{1,2,0:T(2,128)S(1)}, s32[2,16,2]{1,2,0:T(2,128)}, u32[]{:S(2)}) copy-start(s32[2,16,2]{1,2,0:T(2,128)} %param.12) | copy-start | bytes 772
  6.5 143.0 %all-gather.3.cloned.1.call-start = ((), (), s32[]{:S(2)}) async-start(), calls=%async_computation.4 | async-start | bytes 4456448 | tf_op jit(solution)/shard_map/all_gather | solution.py:241
  14.5 47.5 %all-to-all-start = ((bf16[32,2,128,128]{3,2,1,0:T(8,128)(2,1)}), bf16[32,2,128,128]{3,2,1,0:T(8,128)(2,1)S(1)}, u32[]{:S(2)}, u32[]{:S(2)}) async-start(bf16[32,2,128,128]{3,2,1,0:T(8,128)(2,1)} %get-tuple-element.8), calls=%async_computation | async-start | bytes 4194304 | tf_op jit(solution)/shard_map/all_to_all | solution.py:236
  23.9 187.4 %reduce-scatter.2.cloned.1.call-start = ((), (), s32[]{:S(2)}) async-start(), calls=%async_computation.3 | async-start | bytes 2621440 | tf_op jit(solution)/shard_map/reduce_scatter | solution.py:245
  61.9 1.4 copy-start
Sparse Core Ops, SparseCore 0:
  9.1 59.8 all-gather.2
  165.7 45.5 reduce-scatter.1

commit v2 on v1

v2 whole, which is shorter than its diff:
```python
import functools

import jax
import jax.numpy as jnp
from jax import lax
from jax.experimental import pallas as pl
from jax.experimental.pallas import tpu as pltpu
from jax.sharding import PartitionSpec as P

LOG2E = 1.4426950408889634
NT = (((1,), (1,)), ((), ()))
VM = pl.BlockSpec(memory_space=pltpu.VMEM)
SM = pl.BlockSpec(memory_space=pltpu.SMEM)
KB = 4096
BIG = 60 * 2**20
EXTRA = 16
LAG = 2
MESH = pl.DeviceIdType.MESH
ANY = pl.BlockSpec(memory_space=pl.ANY)


def split_queries(rows):
    scale = LOG2E * float(rows.shape[-1]) ** -0.5
    scaled = rows.astype(jnp.float32) * scale
    high = scaled.astype(jnp.bfloat16)
    low = (scaled - high.astype(jnp.float32)).astype(jnp.bfloat16)
    return jnp.concatenate([high, low], axis=1)


def scores_of(keys, split):
    return lax.dot_general(
        jnp.concatenate([keys, keys], axis=1), split, NT, preferred_element_type=jnp.float32
    )


def attend_tile(rows, keys_at, values_t_at, chunks):
    split = split_queries(rows)
    top = total = acc = None
    now = scores_of(keys_at(0), split)
    for c in range(chunks):
        later = scores_of(keys_at(c + 1), split) if c + 1 < chunks else None
        best = jnp.max(now, axis=0, keepdims=True)
        best = best if top is None else jnp.maximum(top, best)
        e = jnp.exp2(now - best)
        part = jnp.sum(e, axis=0, keepdims=True)
        out = jnp.dot(values_t_at(c), e.astype(jnp.bfloat16), preferred_element_type=jnp.float32)
        if top is None:
            acc, total = out, part
        else:
            fade = jnp.exp2(top - best)
            acc, total = acc * fade + out, total * fade + part
        top, now = best, later
    return acc / total, top + jnp.log2(total)


def three_parts(row):
    high = row.astype(jnp.bfloat16).astype(jnp.float32)
    rest = row - high
    mid = rest.astype(jnp.bfloat16).astype(jnp.float32)
    fill = jnp.zeros((EXTRA - 3, row.shape[1]), jnp.float32)
    return jnp.concatenate([high, mid, rest - mid, fill], axis=0).astype(jnp.bfloat16)


def place_kernel(picks_ref, q_ref, out_ref, slot_ref, count_ref):
    heads, blocks, picked = picks_ref.shape
    item = q_ref.shape[1] // blocks
    owners = out_ref.shape[0]
    out_ref[...] = jnp.zeros_like(out_ref)

    def clear(i, _):
        for h in range(heads):
            count_ref[h, i] = 0
        return 0

    lax.fori_loop(0, owners, clear, 0)
    for h in range(heads):

        def one(q, _):
            rows = q_ref[h, pl.ds(pl.multiple_of(q * item, item), item), :]
            for p in range(picked):
                t = picks_ref[h, q, p]
                c = count_ref[h, t]
                count_ref[h, t] = c + 1
                slot_ref[h, q, p] = c
                out_ref[t, h, pl.ds(pl.multiple_of(c * item, item), item), :] = rows
            return 0

        lax.fori_loop(0, blocks, one, 0)


def place(picks, q):
    heads, rows, feature = q.shape
    return pl.pallas_call(
        place_kernel,
        out_shape=(
            jax.ShapeDtypeStruct((32, heads, 128, feature), jnp.bfloat16),
            jax.ShapeDtypeStruct(picks.shape, jnp.int32),
        ),
        in_specs=[SM, VM],
        out_specs=(VM, SM),
        scratch_shapes=[pltpu.SMEM((heads, 32), jnp.int32)],
        compiler_params=pltpu.CompilerParams(vmem_limit_bytes=BIG),
    )(picks, q)


def exchange_kernel(
    out_ref, key_ref, value_ref, q_ref, kv_ref, ret, own_ref, lse_ref,
    keys, values, arrived, done, kvs, acc_ref, top_ref, sum_ref,
    load_sem, send_sem, recv_sem, back_sem, home_sem, kv_send, kv_recv,
):
    owners, heads, slot_rows, feature = out_ref.shape
    spans = kvs.shape[0]
    me = lax.axis_index("seq")
    mine = lax.rem(me, spans)
    group, step = 4, 1024

    loads = [
        pltpu.make_async_copy(key_ref, keys, load_sem.at[0]),
        pltpu.make_async_copy(value_ref, values, load_sem.at[1]),
    ]
    for load in loads:
        load.start()
    barrier = pltpu.get_barrier_semaphore()

    def greet(d, _):
        pl.semaphore_signal(
            barrier, inc=1, device_id={"seq": lax.rem(me + d, owners)}, device_id_type=MESH
        )
        return 0

    lax.fori_loop(1, owners, greet, 0)
    pl.semaphore_wait(barrier, owners - 1)

    def outward(d):
        to = lax.rem(me + d, owners)
        return pltpu.make_async_remote_copy(
            src_ref=out_ref.at[to],
            dst_ref=arrived.at[d],
            send_sem=send_sem.at[d],
            recv_sem=recv_sem.at[d],
            device_id={"seq": to},
            device_id_type=MESH,
        )

    def homeward(d):
        return pltpu.make_async_remote_copy(
            src_ref=done.at[d],
            dst_ref=ret.at[d],
            send_sem=back_sem.at[d],
            recv_sem=home_sem.at[d],
            device_id={"seq": lax.rem(me - d + owners, owners)},
            device_id_type=MESH,
        )

    def kv_copy(d):
        return pltpu.make_async_remote_copy(
            src_ref=kv_ref,
            dst_ref=kvs.at[d],
            send_sem=kv_send.at[d],
            recv_sem=kv_recv.at[d],
            device_id={"seq": lax.rem(me + d, owners)},
            device_id_type=MESH,
        )

    def start_out(d, _):
        outward(d).start()
        return 0

    lax.fori_loop(1, owners, start_out, 0)

    def start_kv(d, _):
        kv_copy(d).start()
        return 0

    lax.fori_loop(1, spans - mine, start_kv, 0)
    arrived[0] = out_ref[me]
    for load in loads:
        load.wait()

    def tile(i, _):
        first = i * group
        for j in range(group):
            if j == 0:

                @pl.when(i > 0)
                def _():
                    outward(first).wait_recv()

            else:
                outward(first + j).wait_recv()
        for h in range(heads):
            rows = jnp.concatenate([arrived[first + j, h] for j in range(group)], axis=0)
            out, lse = attend_tile(
                rows,
                lambda c: keys[h, c * step : (c + 1) * step, :],
                lambda c: values[h, :, c * step : (c + 1) * step],
                KB // step,
            )
            out = out.T.astype(jnp.bfloat16)
            for j in range(group):
                cut = slice(j * slot_rows, (j + 1) * slot_rows)
                done[first + j, h, 0:slot_rows, :] = out[cut, :]
                done[first + j, h, slot_rows : slot_rows + EXTRA, :] = three_parts(lse[:, cut])
        for j in range(group):
            if j == 0:

                @pl.when(i > 0)
                def _():
                    homeward(first).start()

            else:
                homeward(first + j).start()
        return 0

    lax.fori_loop(0, owners // group, tile, 0)
    ret[0] = done[0]

    item = slot_rows // 2
    block_rows = item // 4
    half = kv_ref.shape[2] // 2

    def absorb(pairs, first):
        for h in range(heads):
            split = split_queries(q_ref[h])
            key_rows = [ref[0, h] for ref in pairs]
            key_rows = key_rows[0] if len(pairs) == 1 else jnp.concatenate(key_rows, axis=0)
            value_t = jnp.concatenate(
                [ref[1, h, x : x + half, :] for ref in pairs for x in (0, half)], axis=1
            )
            s = scores_of(key_rows, split)
            if first:
                key_at = lax.broadcasted_iota(jnp.int32, s.shape, 0)
                col = lax.broadcasted_iota(jnp.int32, s.shape, 1)
                row_at = (col // item) * block_rows + lax.rem(col, block_rows)
                s = jnp.where(key_at <= row_at, s, -1e30)
            best = jnp.max(s, axis=0, keepdims=True)
            if not first:
                best = jnp.maximum(top_ref[h, 0:1, :], best)
            e = jnp.exp2(s - best)
            part = jnp.sum(e, axis=0, keepdims=True)
            o = jnp.dot(value_t, e.astype(jnp.bfloat16), preferred_element_type=jnp.float32)
            if first:
                acc_ref[h] = o
                sum_ref[h, 0:1, :] = part
            else:
                fade = jnp.exp2(top_ref[h, 0:1, :] - best)
                acc_ref[h] = acc_ref[h] * fade + o
                sum_ref[h, 0:1, :] = sum_ref[h, 0:1, :] * fade + part
            top_ref[h, 0:1, :] = best

    absorb([kv_ref], True)

    def two(j, _):
        d = 2 * j + 1
        kv_copy(d).wait_recv()
        kv_copy(d + 1).wait_recv()
        absorb([kvs.at[d], kvs.at[d + 1]], False)
        return 0

    lax.fori_loop(0, mine // 2, two, 0)

    @pl.when(lax.rem(mine, 2) == 1)
    def _():
        kv_copy(mine).wait_recv()
        absorb([kvs.at[mine]], False)

    def finish(d, _):
        homeward(d).wait_recv()
        outward(d).wait_send()
        homeward(d).wait_send()
        return 0

    lax.fori_loop(1, owners, finish, 0)

    def finish_kv(d, _):
        kv_copy(d).wait_send()
        return 0

    lax.fori_loop(1, spans - mine, finish_kv, 0)

    for h in range(heads):
        total = sum_ref[h, 0:1, :]
        own_ref[h] = (acc_ref[h] / total).T
        lse_ref[h] = jnp.broadcast_to(top_ref[h, 0:1, :] + jnp.log2(total), lse_ref.shape[1:])


def merge_kernel(picks_ref, slot_ref, own_ref, own_lse_ref, ret, merged_ref):
    owners, heads = ret.shape[:2]
    feature = own_ref.shape[2]
    blocks, picked = picks_ref.shape[1:]
    item = own_ref.shape[1] // blocks
    block_rows = merged_ref.shape[0] // blocks
    fold = item // block_rows
    me = lax.axis_index("seq")
    for h in range(heads):
        own = own_ref[h]
        lses = [own_lse_ref[h, 0:1, :]]
        for p in range(picked):
            pieces = []
            for b in range(blocks):
                at, c = lax.rem(picks_ref[h, b, p] - me + owners, owners), slot_ref[h, b, p]
                lse = jnp.sum(
                    ret[at, h, 2 * item : 2 * item + EXTRA, :].astype(jnp.float32),
                    axis=0,
                    keepdims=True,
                )
                pieces.append(jnp.where(c == 0, lse[:, 0:item], lse[:, item : 2 * item]))
            lses.append(jnp.concatenate(pieces, axis=1))
        best = functools.reduce(jnp.maximum, lses)
        shares = [jnp.exp2(x - best) for x in lses]
        whole = functools.reduce(jnp.add, shares)
        shares = [x / whole for x in shares]
        fill = [jnp.zeros_like(best)] * (8 - len(shares))
        columns = jnp.concatenate(shares + fill, axis=0).T
        for b in range(blocks):
            cut = slice(b * item, (b + 1) * item)
            mix = own[cut, :] * columns[cut, 0:1]
            for p in range(picked):
                at, c = lax.rem(picks_ref[h, b, p] - me + owners, owners), slot_ref[h, b, p]
                got = ret[at, h, pl.ds(pl.multiple_of(c * item, item), item), :]
                mix = mix + got.astype(jnp.float32) * columns[cut, p + 1 : p + 2]
            mix = mix.astype(jnp.bfloat16)
            for g in range(fold):
                lane = (h * fold + g) * feature
                merged_ref[b * block_rows : (b + 1) * block_rows, lane : lane + feature] = mix[
                    g * block_rows : (g + 1) * block_rows, :
                ]


def merge(picks, slots, own, lse, ret):
    return pl.pallas_call(
        merge_kernel,
        out_shape=jax.ShapeDtypeStruct((256, 8 * own.shape[2]), jnp.bfloat16),
        in_specs=[SM, SM, VM, VM, VM],
        out_specs=VM,
        compiler_params=pltpu.CompilerParams(vmem_limit_bytes=BIG),
    )(picks, slots, own, lse, ret)


def exchange(outgoing, keys, values_t, q, kv):
    owners, heads, slot_rows, feature = outgoing.shape
    rows = q.shape[1]
    back = (owners, heads, slot_rows + EXTRA, feature)
    dma = pltpu.SemaphoreType.DMA
    return pl.pallas_call(
        exchange_kernel,
        out_shape=(
            jax.ShapeDtypeStruct(back, jnp.bfloat16),
            jax.ShapeDtypeStruct((heads, rows, feature), jnp.float32),
            jax.ShapeDtypeStruct((heads, 8, rows), jnp.float32),
        ),
        in_specs=[VM, ANY, ANY, VM, VM],
        out_specs=(VM, VM, VM),
        scratch_shapes=[
            pltpu.VMEM(keys.shape, jnp.bfloat16),
            pltpu.VMEM(values_t.shape, jnp.bfloat16),
            pltpu.VMEM(outgoing.shape, jnp.bfloat16),
            pltpu.VMEM(back, jnp.bfloat16),
            pltpu.VMEM((16,) + kv.shape, jnp.bfloat16),
            pltpu.VMEM((heads, feature, rows), jnp.float32),
            pltpu.VMEM((heads, 8, rows), jnp.float32),
            pltpu.VMEM((heads, 8, rows), jnp.float32),
            dma((2,)),
            dma((owners,)),
            dma((owners,)),
            dma((owners,)),
            dma((owners,)),
            dma((16,)),
            dma((16,)),
        ],
        compiler_params=pltpu.CompilerParams(
            collective_id=0, has_side_effects=True, vmem_limit_bytes=BIG
        ),
    )(outgoing, keys, values_t, q, kv)


def project_kernel(
    m_ref, w_ref, out_ref, w_buf, order, sent1, keep, got1, sent2, mine2, got2,
    load_sem, send1, recv1, send2, recv2,
):
    parts, depth, wide = w_buf.shape
    y = lax.axis_index("kvh")
    beside = y + 1 - 2 * lax.rem(y, 2)
    across = 3 - y
    far = 3 - beside
    rows = m_ref.shape[0] // 4

    loads = [
        pltpu.make_async_copy(w_ref.at[:, n * wide : (n + 1) * wide], w_buf.at[n], load_sem.at[n])
        for n in range(parts)
    ]
    for load in loads:
        load.start()
    barrier = pltpu.get_barrier_semaphore()
    for other in (beside, across):
        pl.semaphore_signal(barrier, inc=1, device_id={"kvh": other}, device_id_type=MESH)
    for kind, blocks in enumerate(((beside, far, across, y), (across, far, beside, y))):
        for i, b in enumerate(blocks):
            order[kind, i * rows : (i + 1) * rows, :] = m_ref[
                pl.ds(pl.multiple_of(b * rows, rows), rows), :
            ]
    pl.semaphore_wait(barrier, 2)

    def first_copy(n):
        return pltpu.make_async_remote_copy(
            src_ref=sent1.at[n],
            dst_ref=got1.at[n],
            send_sem=send1.at[n],
            recv_sem=recv1.at[n],
            device_id={"kvh": beside if n % 2 == 0 else across},
            device_id_type=MESH,
        )

    def second_copy(n):
        return pltpu.make_async_remote_copy(
            src_ref=sent2.at[n],
            dst_ref=got2.at[n],
            send_sem=send2.at[n],
            recv_sem=recv2.at[n],
            device_id={"kvh": across if n % 2 == 0 else beside},
            device_id_type=MESH,
        )

    def forward(n):
        first_copy(n).wait_recv()
        both = got1[n].astype(jnp.float32)
        sent2[n] = (keep[n, 0:rows, :] + both[rows:, :]).astype(jnp.bfloat16)
        mine2[n] = keep[n, rows:, :] + both[0:rows, :]
        second_copy(n).start()

    for n in range(parts):
        loads[n].wait()
        product = jnp.dot(order[n % 2], w_buf[n], preferred_element_type=jnp.float32)
        sent1[n] = product[0 : 2 * rows, :].astype(jnp.bfloat16)
        keep[n] = product[2 * rows :, :]
        first_copy(n).start()
        if n >= LAG:
            forward(n - LAG)
    for n in range(parts - LAG, parts):
        forward(n)
    for n in range(parts):
        second_copy(n).wait_recv()
        out_ref[:, n * wide : (n + 1) * wide] = (
            mine2[n] + got2[n].astype(jnp.float32)
        ).astype(jnp.bfloat16)
    for n in range(parts):
        first_copy(n).wait_send()
        second_copy(n).wait_send()


def project(merged, weight):
    rows, depth = merged.shape
    width = weight.shape[1]
    parts = 8
    wide = width // parts
    quarter = rows // 4
    dma = pltpu.SemaphoreType.DMA
    return pl.pallas_call(
        project_kernel,
        out_shape=jax.ShapeDtypeStruct((quarter, width), jnp.bfloat16),
        in_specs=[VM, ANY],
        out_specs=VM,
        scratch_shapes=[
            pltpu.VMEM((parts, depth, wide), jnp.bfloat16),
            pltpu.VMEM((2, rows, depth), jnp.bfloat16),
            pltpu.VMEM((parts, 2 * quarter, wide), jnp.bfloat16),
            pltpu.VMEM((parts, 2 * quarter, wide), jnp.float32),
            pltpu.VMEM((parts, 2 * quarter, wide), jnp.bfloat16),
            pltpu.VMEM((parts, quarter, wide), jnp.bfloat16),
            pltpu.VMEM((parts, quarter, wide), jnp.float32),
            pltpu.VMEM((parts, quarter, wide), jnp.bfloat16),
            dma((parts,)),
            dma((parts,)),
            dma((parts,)),
            dma((parts,)),
            dma((parts,)),
        ],
        compiler_params=pltpu.CompilerParams(
            collective_id=1, has_side_effects=True, vmem_limit_bytes=BIG
        ),
    )(merged, weight)


def on_device(queries, ctx_keys, ctx_values, new_keys, new_values, picks, out_weight):
    q = queries.reshape(16, 16, 2, 4, 128).transpose(2, 0, 3, 1, 4).reshape(2, 1024, 128)
    outgoing, slots = place(picks, q)
    keys = ctx_keys.transpose(1, 0, 2)
    values_t = ctx_values.transpose(1, 2, 0)
    new_t = new_values.reshape(2, 128, 2, 128).transpose(2, 0, 3, 1).reshape(2, 256, 128)
    kv = jnp.stack([new_keys.transpose(1, 0, 2), new_t])
    ret, own, lse = exchange(outgoing, keys, values_t, q, kv)
    merged = merge(picks, slots, own, lse, ret)
    return project(merged, out_weight)


def solution(mesh):
    placed = (
        P("seq", "kvh", None),
        P("seq", "kvh", None),
        P("seq", "kvh", None),
        P("seq", "kvh", None),
        P("seq", "kvh", None),
        P("kvh", "seq", None),
        P("kvh", None),
    )
    return jax.shard_map(
        on_device, mesh=mesh, in_specs=placed, out_specs=P(("seq", "kvh"), None), check_vma=False
    )
```

time: 219 us -> 175 us (0.80)
  Pallas kernels: 58.7 us -> 160 us
  waiting for transfers between devices: 74.3 us -> 0 us
  blocking collectives: 39.8 us -> 0 us
  between operations: 13.4 us -> 0.06 us
  starting transfers between devices: 9.49 us -> 0 us
  matrix products: 7.24 us -> 0 us
    pallas_call x2 -> x3, Pallas kernels: 55.2 us -> 156 us  [the longest x1 126 us: exchange(): pl.pallas_call(exchange_kernel, out_shape=(jax.ShapeDtypeStruct(back, jnp...]
    reduce_scatter x1 -> x0, waiting for transfers between devices: 45.7 us -> none  [on_device(): lax.psum_scatter(jnp.dot(merged, out_weight, preferred_element_type=jnp.f...]
    all_to_all x1 -> x0, blocking collectives: 39.8 us -> none  [on_device(): ret = lax.all_to_all(done, 'seq', split_axis=0, concat_axis=0, tiled=True)]
    all_to_all x1 -> x0, waiting for transfers between devices: 28.5 us -> none  [on_device(): lax.all_to_all(outgoing, 'seq', split_axis=0, concat_axis=0, tiled=True)]
    all_to_all x1 -> x0, starting transfers between devices: 9.45 us -> none  [on_device(): lax.all_to_all(outgoing, 'seq', split_axis=0, concat_axis=0, tiled=True)]
    dot_general x1 -> x0, matrix products: 7.24 us -> none  [on_device(): jnp.dot(merged, out_weight, preferred_element_type=jnp.float32)]
    unnamed x7 -> x11, local copies, waits for them, and re-layouts: 11.5 us -> 10.6 us
  transfers between devices with their start and end apart: 3 -> 0, of which waited for: 2 -> 0; matrix products, arithmetic and copies ran while one was open for 6% -> 0% of each run, Pallas kernels for 23% -> 0%
where the time goes in v2:
time: 175 us; the launch traced here: 173 us
  Pallas kernels  160 us (91%)
  local copies, waits for them, and re-layouts  12.7 us (7%)
    pallas_call x1, Pallas kernels, exchange(): pl.pallas_call(exchange_kernel, out_shape=(jax.ShapeDtypeStruct(back, jnp...  126 us
    pallas_call x1, Pallas kernels, project(): pl.pallas_call(project_kernel, out_shape=jax.ShapeDtypeStruct((quarter, w...  25 us
    unnamed x11, local copies, waits for them, and re-layouts  10.6 us
    pallas_call x1, Pallas kernels, merge(): pl.pallas_call(merge_kernel, out_shape=jax.ShapeDtypeStruct((256, 8 * own...  4.75 us

profile of v2, /device:TPU:1, one launch (start us, length us, event | category | flops | bytes accessed | tf_op | source)
XLA Modules:
  0.0 173.1 jit_solution(10823866627625610806)
XLA Ops:
  0.0 1.4 copy.14.picks_ref
  1.4 2.0 %copy.8 = bf16[16,16,2,4,128]{4,1,3,0,2:T(8,128)(2,1)} copy(bf16[16,16,2,4,128]{4,3,2,1,0:T(4,128)(2,1)} %bitcast.21) | data formatting | bytes 1048576 | tf_op jit(solution)/shard_map/reshape | solution.py:485
  3.3 3.4 %shard_map.73 = (bf16[32,2,128,128]{3,2,1,0:T(8,128)(2,1)}, s32[2,16,2]{2,1,0:T(8,128)}) custom-call(s32[2,16,2]{2,1,0:T(8,128)} %copy.14.picks_ref, bf16[2,1024,128]{2,1,0:T(8,128)(2,1)} %bitcast.19), custom_call_target="tpu_custom_call" | custom-call | tf_op jit(solution)/shard_map/pallas_call | solution.py:93
  6.8 0.0 copy-start
  6.8 3.4 %copy.17 = bf16[4096,2,128]{2,0,1:T(8,128)(2,1)} copy(bf16[4096,2,128]{2,1,0:T(2,128)(2,1)} %param.8) | data formatting | bytes 4194304 | tf_op args[1]
  10.1 0.0 copy-done
  10.1 0.0 copy-start.1
  10.1 0.0 copy-start.2
  10.2 3.9 %copy.11 = bf16[4096,2,128]{0,2,1:T(8,128)(2,1)} copy(bf16[4096,2,128]{2,1,0:T(2,128)(2,1)S(1)} %copy-done) | data formatting | bytes 4194304 | tf_op args[2]
  14.1 0.0 copy-done.1
  14.1 0.1 copy.13
  14.2 0.0 copy-done.2
  14.3 0.7 pad_maximum_fusion.kv_ref
  15.0 126.5 %shard_map.74 = (bf16[32,2,144,128]{3,2,1,0:T(8,128)(2,1)}, f32[2,1024,128]{2,1,0:T(8,128)}, f32[2,8,1024]{2,1,0:T(8,128)}) custom-call(bf16[32,2,128,128]{3,2,1,0:T(8,128)(2,1)} %get-tuple-element.11.out_ref, bf16[2,4096,128]{2,1,0:T(8,128)(2,1)} %bitcast.17, bf16[2,128,4096]{2,1,0:T(8,128)(2,1)} %bitcast.18, bf16[2,1024,128]{2,1,0:T(8,128)(2,1)} %bitcast.20, ...), custom_call_target="tpu_custom_call" | custom-call | tf_op jit(solution)/shard_map/pallas_call | solution.py:345
  141.5 4.7 %shard_map.75.m_ref = bf16[256,1024]{1,0:T(8,128)(2,1)} custom-call(s32[2,16,2]{2,1,0:T(8,128)} %copy.14.picks_ref, s32[2,16,2]{2,1,0:T(8,128)} %get-tuple-element.10.slot_ref, f32[2,1024,128]{2,1,0:T(8,128)} %get-tuple-element.12.own_ref, f32[2,8,1024]{2,1,0:T(8,128)} %get-tuple-element.13.own_lse_ref, bf16[32,2,144,128]{3,2,1,0:T(8,128)(2,1)} %get-tuple-element.14.ret), custom_call_target="tpu_custom_call" | custom-call | tf_op jit(solution)/shard_map/pallas_call | solution.py:331
  146.2 25.0 %shard_map.76 = bf16[64,4096]{1,0:T(8,128)(2,1)} custom-call(bf16[256,1024]{1,0:T(8,128)(2,1)} %shard_map.75.m_ref, bf16[1024,4096]{1,0:T(8,128)(2,1)} %w_ref.1), custom_call_target="tpu_custom_call" | custom-call | tf_op jit(solution)/shard_map/pallas_call | solution.py:458
  171.2 1.9 %copy.20 = bf16[64,4096]{1,0:T(8,128)(2,1)} copy(bf16[64,4096]{1,0:T(8,128)(2,1)} %shard_map.76) | data formatting | bytes 1048576
  (1 shorter events, 0.0 us)
Async XLA Ops:
  6.8 3.4 %copy-start = (bf16[4096,2,128]{2,1,0:T(2,128)(2,1)S(1)}, bf16[4096,2,128]{2,1,0:T(2,128)(2,1)}, u32[]{:S(2)}) copy-start(bf16[4096,2,128]{2,1,0:T(2,128)(2,1)} %param.9) | copy-start | bytes 6291460
  10.1 3.9 %copy-start.1 = (bf16[256,2,128]{2,1,0:T(2,128)(2,1)S(1)}, bf16[256,2,128]{2,1,0:T(2,128)(2,1)}, u32[]{:S(2)}) copy-start(bf16[256,2,128]{2,1,0:T(2,128)(2,1)} %param.11) | copy-start | bytes 393220
  10.1 4.1 %copy-start.2 = (bf16[256,2,128]{2,1,0:T(2,128)(2,1)S(1)}, bf16[256,2,128]{2,1,0:T(2,128)(2,1)}, u32[]{:S(2)}) copy-start(bf16[256,2,128]{2,1,0:T(2,128)(2,1)} %param.10) | copy-start | bytes 393220

commit v3 on v2

--- a/solution.py
+++ b/solution.py
@@ -9,6 +9,7 @@
 
 LOG2E = 1.4426950408889634
 NT = (((1,), (1,)), ((), ()))
+TN = (((0,), (0,)), ((), ()))
 VM = pl.BlockSpec(memory_space=pltpu.VMEM)
 SM = pl.BlockSpec(memory_space=pltpu.SMEM)
 KB = 4096
@@ -53,12 +54,37 @@
     return acc / total, top + jnp.log2(total)
 
 
-def three_parts(row):
-    high = row.astype(jnp.bfloat16).astype(jnp.float32)
-    rest = row - high
-    mid = rest.astype(jnp.bfloat16).astype(jnp.float32)
-    fill = jnp.zeros((EXTRA - 3, row.shape[1]), jnp.float32)
-    return jnp.concatenate([high, mid, rest - mid, fill], axis=0).astype(jnp.bfloat16)
+def three_parts(rows):
+    parts = []
+    for row in rows:
+        high = row.astype(jnp.bfloat16).astype(jnp.float32)
+        rest = row - high
+        mid = rest.astype(jnp.bfloat16).astype(jnp.float32)
+        parts += [high, mid, rest - mid]
+    fill = jnp.zeros((EXTRA - len(parts), rows[0].shape[1]), jnp.float32)
+    return jnp.concatenate(parts + [fill], axis=0).astype(jnp.bfloat16)
+
+
+CHIPS = (
+    ((0, 0), (0, 1)), ((1, 0), (0, 3)), ((3, 0), (1, 1)), ((3, 3), (1, 3)),
+    ((3, 1), (0, 2)), ((2, 0), (1, 2)), ((2, 1), (3, 2)), ((2, 3), (2, 2)),
+)
+DIGITS = tuple(
+    sum(pair[a][b] * 4**i for i, pair in enumerate(CHIPS)) for a in range(2) for b in range(2)
+)
+
+
+def offsets_of(digits):
+    za, xa, zb, xb = [lax.rem(x, 4) for x in digits]
+    return ((za, xa, 0), (za, xa, 1), (zb, xb, 0), (zb, xb, 1))
+
+
+def next_digits(digits):
+    return tuple(lax.div(x, 4) for x in digits)
+
+
+def first_digits():
+    return tuple(jnp.int32(x) for x in DIGITS)
 
 
 def place_kernel(picks_ref, q_ref, out_ref, slot_ref, count_ref):
@@ -105,18 +131,19 @@
 
 def exchange_kernel(
     out_ref, key_ref, value_ref, q_ref, kv_ref, ret, own_ref, lse_ref,
-    keys, values, arrived, done, kvs, acc_ref, top_ref, sum_ref,
-    load_sem, send_sem, recv_sem, back_sem, home_sem, kv_send, kv_recv,
+    raw, keys, values, arrived, done, kvs, acc_ref, top_ref, sum_ref,
+    load_sem, send_sem, recv_sem, back_sem, home_sem, kv_send, kv_recv, fwd_send, fwd_recv,
 ):
     owners, heads, slot_rows, feature = out_ref.shape
-    spans = kvs.shape[0]
     me = lax.axis_index("seq")
-    mine = lax.rem(me, spans)
+    z, x, core = lax.div(me, 8), lax.rem(lax.div(me, 2), 4), lax.rem(me, 2)
+    sibling = me + 1 - 2 * core
+    place = lax.rem(z, 2) * 4 + x
     group, step = 4, 1024
 
     loads = [
-        pltpu.make_async_copy(key_ref, keys, load_sem.at[0]),
-        pltpu.make_async_copy(value_ref, values, load_sem.at[1]),
+        pltpu.make_async_copy(key_ref, raw.at[0], load_sem.at[0]),
+        pltpu.make_async_copy(value_ref, raw.at[1], load_sem.at[1]),
     ]
     for load in loads:
         load.start()
@@ -129,65 +156,138 @@
         return 0
 
     lax.fori_loop(1, owners, greet, 0)
-    pl.semaphore_wait(barrier, owners - 1)
-
-    def outward(d):
-        to = lax.rem(me + d, owners)
+
+    def ahead(offset):
+        dz, dx, dc = offset
+        return lax.rem(z + dz, 4) * 8 + lax.rem(x + dx, 4) * 2 + lax.rem(core + dc, 2)
+
+    def behind(offset):
+        dz, dx, dc = offset
+        return lax.rem(z + 4 - dz, 4) * 8 + lax.rem(x + 4 - dx, 4) * 2 + lax.rem(core + dc, 2)
+
+    def outward(k, to):
         return pltpu.make_async_remote_copy(
             src_ref=out_ref.at[to],
-            dst_ref=arrived.at[d],
-            send_sem=send_sem.at[d],
-            recv_sem=recv_sem.at[d],
+            dst_ref=arrived.at[k],
+            send_sem=send_sem.at[k],
+            recv_sem=recv_sem.at[k],
             device_id={"seq": to},
             device_id_type=MESH,
         )
 
-    def homeward(d):
+    def homeward(k, to):
         return pltpu.make_async_remote_copy(
-            src_ref=done.at[d],
-            dst_ref=ret.at[d],
-            send_sem=back_sem.at[d],
-            recv_sem=home_sem.at[d],
-            device_id={"seq": lax.rem(me - d + owners, owners)},
+            src_ref=done.at[k],
+            dst_ref=ret.at[k],
+            send_sem=back_sem.at[k],
+            recv_sem=home_sem.at[k],
+            device_id={"seq": to},
             device_id_type=MESH,
         )
 
     def kv_copy(d):
         return pltpu.make_async_remote_copy(
             src_ref=kv_ref,
-            dst_ref=kvs.at[d],
+            dst_ref=kvs.at[2 * d + core],
             send_sem=kv_send.at[d],
             recv_sem=kv_recv.at[d],
-            device_id={"seq": lax.rem(me + d, owners)},
+            device_id={"seq": lax.rem(me + 2 * d, owners)},
             device_id_type=MESH,
         )
 
-    def start_out(d, _):
-        outward(d).start()
-        return 0
-
-    lax.fori_loop(1, owners, start_out, 0)
+    def kv_beside():
+        return pltpu.make_async_remote_copy(
+            src_ref=kv_ref,
+            dst_ref=kvs.at[0],
+            send_sem=kv_send.at[0],
+            recv_sem=kv_recv.at[0],
+            device_id={"seq": sibling},
+            device_id_type=MESH,
+        )
+
+    def kv_forward(d, from_core):
+        return pltpu.make_async_remote_copy(
+            src_ref=kvs.at[2 * d + from_core],
+            dst_ref=kvs.at[2 * d + from_core],
+            send_sem=fwd_send.at[d],
+            recv_sem=fwd_recv.at[d],
+            device_id={"seq": sibling},
+            device_id_type=MESH,
+        )
+
+    span = 2 * feature
+    row = lax.broadcasted_iota(jnp.int32, (span, span), 0)
+    col = lax.broadcasted_iota(jnp.int32, (span, span), 1)
+    picking = (col == 2 * lax.rem(row, feature) + lax.div(row, feature)).astype(jnp.bfloat16)
+    placing = (row == 2 * lax.rem(col, feature) + lax.div(col, feature)).astype(jnp.bfloat16)
+
+    pl.semaphore_wait(barrier, owners - 1)
+
+    def start_out(i, digits):
+        for j, offset in enumerate(offsets_of(digits)):
+            k = i * group + j
+            if j == 0:
+
+                @pl.when(i > 0)
+                def _():
+                    outward(k, ahead(offset)).start()
+
+            else:
+                outward(k, ahead(offset)).start()
+        return next_digits(digits)
+
+    lax.fori_loop(0, owners // group, start_out, first_digits())
 
     def start_kv(d, _):
         kv_copy(d).start()
         return 0
 
-    lax.fori_loop(1, spans - mine, start_kv, 0)
+    lax.fori_loop(1, 8 - place, start_kv, 0)
+
+    @pl.when(core == 0)
+    def _():
+        kv_beside().start()
+
     arrived[0] = out_ref[me]
-    for load in loads:
-        load.wait()
-
-    def tile(i, _):
+    loads[0].wait()
+
+    def sort_keys(j, _):
+        block = raw[0, pl.ds(pl.multiple_of(j * span, span), span), :]
+        both = jnp.dot(picking, block, preferred_element_type=jnp.float32).astype(jnp.bfloat16)
+        for h in range(heads):
+            keys[h, pl.ds(pl.multiple_of(j * feature, feature), feature), :] = both[
+                h * feature : (h + 1) * feature, :
+            ]
+        return 0
+
+    lax.fori_loop(0, KB // feature, sort_keys, 0, unroll=4)
+    loads[1].wait()
+
+    def sort_values(j, _):
+        block = raw[1, pl.ds(pl.multiple_of(j * span, span), span), :]
+        both = lax.dot_general(block, placing, TN, preferred_element_type=jnp.float32)
+        both = both.astype(jnp.bfloat16)
+        for h in range(heads):
+            values[h, :, pl.ds(pl.multiple_of(j * feature, feature), feature)] = both[
+                :, h * feature : (h + 1) * feature
+            ]
+        return 0
+
+    lax.fori_loop(0, KB // feature, sort_values, 0, unroll=4)
+
+    def tile(i, digits):
         first = i * group
-        for j in range(group):
+        offsets = offsets_of(digits)
+        for j, offset in enumerate(offsets):
             if j == 0:
 
                 @pl.when(i > 0)
                 def _():
-                    outward(first).wait_recv()
+                    outward(first, sibling).wait_recv()
 
             else:
-                outward(first + j).wait_recv()
+                outward(first + j, sibling).wait_recv()
+        lses = []
         for h in range(heads):
             rows = jnp.concatenate([arrived[first + j, h] for j in range(group)], axis=0)
             out, lse = attend_tile(
@@ -197,27 +297,38 @@
                 KB // step,
             )
             out = out.T.astype(jnp.bfloat16)
+            lses.append(lse)
             for j in range(group):
                 cut = slice(j * slot_rows, (j + 1) * slot_rows)
-                done[first + j, h, 0:slot_rows, :] = out[cut, :]
-                done[first + j, h, slot_rows : slot_rows + EXTRA, :] = three_parts(lse[:, cut])
-        for j in range(group):
+                done[first + j, h * slot_rows : (h + 1) * slot_rows, :] = out[cut, :]
+        for j, offset in enumerate(offsets):
+            cut = slice(j * slot_rows, (j + 1) * slot_rows)
+            done[first + j, heads * slot_rows : heads * slot_rows + EXTRA, :] = three_parts(
+                [lse[:, cut] for lse in lses]
+            )
             if j == 0:
 
                 @pl.when(i > 0)
                 def _():
-                    homeward(first).start()
+                    homeward(first, behind(offset)).start()
 
             else:
-                homeward(first + j).start()
-        return 0
-
-    lax.fori_loop(0, owners // group, tile, 0)
+                homeward(first + j, behind(offset)).start()
+        return next_digits(digits)
+
+    lax.fori_loop(0, owners // group, tile, first_digits())
     ret[0] = done[0]
 
     item = slot_rows // 2
     block_rows = item // 4
     half = kv_ref.shape[2] // 2
+
+    def pass_on(d, _):
+        kv_copy(d).wait_recv()
+        kv_forward(d, core).start()
+        return 0
+
+    lax.fori_loop(1, place + 1, pass_on, 0)
 
     def absorb(pairs, first):
         for h in range(heads):
@@ -225,13 +336,13 @@
             key_rows = [ref[0, h] for ref in pairs]
             key_rows = key_rows[0] if len(pairs) == 1 else jnp.concatenate(key_rows, axis=0)
             value_t = jnp.concatenate(
-                [ref[1, h, x : x + half, :] for ref in pairs for x in (0, half)], axis=1
+                [ref[1, h, at : at + half, :] for ref in pairs for at in (0, half)], axis=1
             )
             s = scores_of(key_rows, split)
             if first:
                 key_at = lax.broadcasted_iota(jnp.int32, s.shape, 0)
-                col = lax.broadcasted_iota(jnp.int32, s.shape, 1)
-                row_at = (col // item) * block_rows + lax.rem(col, block_rows)
+                lane = lax.broadcasted_iota(jnp.int32, s.shape, 1)
+                row_at = (lane // item) * block_rows + lax.rem(lane, block_rows)
                 s = jnp.where(key_at <= row_at, s, -1e30)
             best = jnp.max(s, axis=0, keepdims=True)
             if not first:
@@ -250,59 +361,72 @@
 
     absorb([kv_ref], True)
 
-    def two(j, _):
-        d = 2 * j + 1
-        kv_copy(d).wait_recv()
-        kv_copy(d + 1).wait_recv()
-        absorb([kvs.at[d], kvs.at[d + 1]], False)
-        return 0
-
-    lax.fori_loop(0, mine // 2, two, 0)
-
-    @pl.when(lax.rem(mine, 2) == 1)
+    @pl.when(core == 1)
     def _():
-        kv_copy(mine).wait_recv()
-        absorb([kvs.at[mine]], False)
-
-    def finish(d, _):
-        homeward(d).wait_recv()
-        outward(d).wait_send()
-        homeward(d).wait_send()
-        return 0
-
-    lax.fori_loop(1, owners, finish, 0)
-
-    def finish_kv(d, _):
-        kv_copy(d).wait_send()
-        return 0
-
-    lax.fori_loop(1, spans - mine, finish_kv, 0)
-
+        kv_beside().wait_recv()
+        absorb([kvs.at[0]], False)
+
+    def two(d, _):
+        kv_forward(d, core).wait_recv()
+        absorb([kvs.at[2 * d], kvs.at[2 * d + 1]], False)
+        return 0
+
+    lax.fori_loop(1, place + 1, two, 0)
     for h in range(heads):
         total = sum_ref[h, 0:1, :]
         own_ref[h] = (acc_ref[h] / total).T
         lse_ref[h] = jnp.broadcast_to(top_ref[h, 0:1, :] + jnp.log2(total), lse_ref.shape[1:])
 
-
-def merge_kernel(picks_ref, slot_ref, own_ref, own_lse_ref, ret, merged_ref):
-    owners, heads = ret.shape[:2]
+    def finish(k, _):
+        homeward(k, sibling).wait_recv()
+        outward(k, sibling).wait_send()
+        homeward(k, sibling).wait_send()
+        return 0
+
+    lax.fori_loop(1, owners, finish, 0)
+
+    def finish_kv(d, _):
+        kv_copy(d).wait_send()
+        return 0
+
+    lax.fori_loop(1, 8 - place, finish_kv, 0)
+
+    @pl.when(core == 0)
+    def _():
+        kv_beside().wait_send()
+
+    def finish_forward(d, _):
+        kv_forward(d, core).wait_send()
+        return 0
+
+    lax.fori_loop(1, place + 1, finish_forward, 0)
+
+
+def merge_kernel(picks_ref, slot_ref, table_ref, own_ref, own_lse_ref, ret, merged_ref):
+    heads = own_ref.shape[0]
     feature = own_ref.shape[2]
     blocks, picked = picks_ref.shape[1:]
     item = own_ref.shape[1] // blocks
     block_rows = merged_ref.shape[0] // blocks
     fold = item // block_rows
     me = lax.axis_index("seq")
+    z, x, core = lax.div(me, 8), lax.rem(lax.div(me, 2), 4), lax.rem(me, 2)
+
+    def place_of(t):
+        dz = lax.rem(lax.div(t, 8) - z + 4, 4)
+        dx = lax.rem(lax.rem(lax.div(t, 2), 4) - x + 4, 4)
+        return 2 * table_ref[dz, dx] + lax.rem(lax.rem(t, 2) - core + 2, 2)
+
     for h in range(heads):
         own = own_ref[h]
         lses = [own_lse_ref[h, 0:1, :]]
         for p in range(picked):
             pieces = []
             for b in range(blocks):
-                at, c = lax.rem(picks_ref[h, b, p] - me + owners, owners), slot_ref[h, b, p]
+                at, c = place_of(picks_ref[h, b, p]), slot_ref[h, b, p]
+                extra = ret[at, heads * 2 * item : heads * 2 * item + EXTRA, :]
                 lse = jnp.sum(
-                    ret[at, h, 2 * item : 2 * item + EXTRA, :].astype(jnp.float32),
-                    axis=0,
-                    keepdims=True,
+                    extra.astype(jnp.float32)[3 * h : 3 * h + 3, :], axis=0, keepdims=True
                 )
                 pieces.append(jnp.where(c == 0, lse[:, 0:item], lse[:, item : 2 * item]))
             lses.append(jnp.concatenate(pieces, axis=1))
@@ -316,8 +440,8 @@
             cut = slice(b * item, (b + 1) * item)
             mix = own[cut, :] * columns[cut, 0:1]
             for p in range(picked):
-                at, c = lax.rem(picks_ref[h, b, p] - me + owners, owners), slot_ref[h, b, p]
-                got = ret[at, h, pl.ds(pl.multiple_of(c * item, item), item), :]
+                at, c = place_of(picks_ref[h, b, p]), slot_ref[h, b, p]
+                got = ret[at, pl.ds(pl.multiple_of((2 * h + c) * item, item), item), :]
                 mix = mix + got.astype(jnp.float32) * columns[cut, p + 1 : p + 2]
             mix = mix.astype(jnp.bfloat16)
             for g in range(fold):
@@ -328,19 +452,24 @@
 
 
 def merge(picks, slots, own, lse, ret):
+    table = [[0] * 4 for _ in range(4)]
+    for i, pair in enumerate(CHIPS):
+        for j, (dz, dx) in enumerate(pair):
+            table[dz][dx] = 2 * i + j
+    table = jnp.array(table, jnp.int32)
     return pl.pallas_call(
         merge_kernel,
         out_shape=jax.ShapeDtypeStruct((256, 8 * own.shape[2]), jnp.bfloat16),
-        in_specs=[SM, SM, VM, VM, VM],
+        in_specs=[SM, SM, SM, VM, VM, VM],
         out_specs=VM,
         compiler_params=pltpu.CompilerParams(vmem_limit_bytes=BIG),
-    )(picks, slots, own, lse, ret)
-
-
-def exchange(outgoing, keys, values_t, q, kv):
+    )(picks, slots, table, own, lse, ret)
+
+
+def exchange(outgoing, keys, values, q, kv):
     owners, heads, slot_rows, feature = outgoing.shape
     rows = q.shape[1]
-    back = (owners, heads, slot_rows + EXTRA, feature)
+    back = (owners, heads * slot_rows + EXTRA, feature)
     dma = pltpu.SemaphoreType.DMA
     return pl.pallas_call(
         exchange_kernel,
@@ -352,8 +481,9 @@
         in_specs=[VM, ANY, ANY, VM, VM],
         out_specs=(VM, VM, VM),
         scratch_shapes=[
-            pltpu.VMEM(keys.shape, jnp.bfloat16),
-            pltpu.VMEM(values_t.shape, jnp.bfloat16),
+            pltpu.VMEM((2,) + keys.shape, jnp.bfloat16),
+            pltpu.VMEM((heads, KB, feature), jnp.bfloat16),
+            pltpu.VMEM((heads, feature, KB), jnp.bfloat16),
             pltpu.VMEM(outgoing.shape, jnp.bfloat16),
             pltpu.VMEM(back, jnp.bfloat16),
             pltpu.VMEM((16,) + kv.shape, jnp.bfloat16),
@@ -365,13 +495,15 @@
             dma((owners,)),
             dma((owners,)),
             dma((owners,)),
-            dma((16,)),
-            dma((16,)),
+            dma((8,)),
+            dma((8,)),
+            dma((8,)),
+            dma((8,)),
         ],
         compiler_params=pltpu.CompilerParams(
             collective_id=0, has_side_effects=True, vmem_limit_bytes=BIG
         ),
-    )(outgoing, keys, values_t, q, kv)
+    )(outgoing, keys, values, q, kv)
 
 
 def project_kernel(
@@ -484,11 +616,11 @@
 def on_device(queries, ctx_keys, ctx_values, new_keys, new_values, picks, out_weight):
     q = queries.reshape(16, 16, 2, 4, 128).transpose(2, 0, 3, 1, 4).reshape(2, 1024, 128)
     outgoing, slots = place(picks, q)
-    keys = ctx_keys.transpose(1, 0, 2)
-    values_t = ctx_values.transpose(1, 2, 0)
+    keys = ctx_keys.reshape(8192, 128)
+    values = ctx_values.reshape(8192, 128)
     new_t = new_values.reshape(2, 128, 2, 128).transpose(2, 0, 3, 1).reshape(2, 256, 128)
     kv = jnp.stack([new_keys.transpose(1, 0, 2), new_t])
-    ret, own, lse = exchange(outgoing, keys, values_t, q, kv)
+    ret, own, lse = exchange(outgoing, keys, values, q, kv)
     merged = merge(picks, slots, own, lse, ret)
     return project(merged, out_weight)
 

time: 175 us -> 137 us (0.78)
  Pallas kernels: 160 us -> 127 us
  local copies, waits for them, and re-layouts: 12.7 us -> 7.14 us
    pallas_call x1, Pallas kernels: 126 us -> 92.2 us  [exchange(): pl.pallas_call(exchange_kernel, out_shape=(jax.ShapeDtypeStruct(back, jnp...]
    unnamed x11 -> x3, local copies, waits for them, and re-layouts: 10.6 us -> 4.15 us
where the time goes in v3:
time: 137 us; the launch traced here: 135 us
  Pallas kernels  127 us (93%)
  local copies, waits for them, and re-layouts  7.14 us (5%)
    pallas_call x1, Pallas kernels, exchange(): pl.pallas_call(exchange_kernel, out_shape=(jax.ShapeDtypeStruct(back, jnp...  92.2 us
    pallas_call x1, Pallas kernels, project(): pl.pallas_call(project_kernel, out_shape=jax.ShapeDtypeStruct((quarter, w...  25.7 us
    pallas_call x1, Pallas kernels, merge(): pl.pallas_call(merge_kernel, out_shape=jax.ShapeDtypeStruct((256, 8 * own...  5.44 us
    unnamed x3, local copies, waits for them, and re-layouts  4.15 us
    pallas_call x1, Pallas kernels, place(): pl.pallas_call(place_kernel, out_shape=(jax.ShapeDtypeStruct((32, heads,...  3.44 us

profile of v3, /device:TPU:1, one launch (start us, length us, event | category | flops | bytes accessed | tf_op | source)
XLA Modules:
  0.0 134.8 jit_solution(15381009809204420637)
XLA Ops:
  0.0 1.4 %copy.13.picks_ref = s32[2,16,2]{2,1,0:T(8,128)} copy(s32[2,16,2]{1,2,0:T(2,128)} %param.13) | data formatting | bytes 512 | tf_op args[5]
  1.4 0.9 copy.15
  2.3 1.0 copy.12
  3.3 0.7 pad_maximum_fusion.kv_ref
  4.1 2.0 %copy.9 = bf16[16,16,2,4,128]{4,1,3,0,2:T(8,128)(2,1)} copy(bf16[16,16,2,4,128]{4,3,2,1,0:T(4,128)(2,1)} %bitcast.19) | data formatting | bytes 1048576 | tf_op jit(solution)/shard_map/reshape | solution.py:617
  6.0 3.4 %shard_map.82 = (bf16[32,2,128,128]{3,2,1,0:T(8,128)(2,1)}, s32[2,16,2]{2,1,0:T(8,128)}) custom-call(s32[2,16,2]{2,1,0:T(8,128)} %copy.13.picks_ref, bf16[2,1024,128]{2,1,0:T(8,128)(2,1)} %bitcast.15), custom_call_target="tpu_custom_call" | custom-call | tf_op jit(solution)/shard_map/pallas_call | solution.py:119
  9.5 92.2 %shard_map.83 = (bf16[32,272,128]{2,1,0:T(8,128)(2,1)}, f32[2,1024,128]{2,1,0:T(8,128)}, f32[2,8,1024]{2,1,0:T(8,128)}) custom-call(bf16[32,2,128,128]{3,2,1,0:T(8,128)(2,1)} %get-tuple-element.11.out_ref, bf16[8192,128]{1,0:T(8,128)(2,1)} %bitcast.17, bf16[8192,128]{1,0:T(8,128)(2,1)} %bitcast.18, bf16[2,1024,128]{2,1,0:T(8,128)(2,1)} %bitcast.16, ...), custom_call_target="tpu_custom_call" | custom-call | tf_op jit(solution)/shard_map/pallas_call | solution.py:474
  101.7 5.4 %shard_map.84.m_ref = bf16[256,1024]{1,0:T(8,128)(2,1)} custom-call(s32[2,16,2]{2,1,0:T(8,128)} %copy.13.picks_ref, s32[2,16,2]{2,1,0:T(8,128)} %get-tuple-element.10.slot_ref, s32[4,4]{1,0:T(4,128)} %constant.2.clone.table_ref, f32[2,1024,128]{2,1,0:T(8,128)} %get-tuple-element.12.own_ref, f32[2,8,1024]{2,1,0:T(8,128)} %get-tuple-element.13.own_lse_ref, ...), custom_call_target="tpu_custom_call" | custom-call | tf_op jit(solution)/shard_map/pallas_call | solution.py:460
  107.1 25.7 %shard_map.85 = bf16[64,4096]{1,0:T(8,128)(2,1)} custom-call(bf16[256,1024]{1,0:T(8,128)(2,1)} %shard_map.84.m_ref, bf16[1024,4096]{1,0:T(8,128)(2,1)} %w_ref.1), custom_call_target="tpu_custom_call" | custom-call | tf_op jit(solution)/shard_map/pallas_call | solution.py:590
  132.9 1.9 %copy.17 = bf16[64,4096]{1,0:T(8,128)(2,1)} copy(bf16[64,4096]{1,0:T(8,128)(2,1)} %shard_map.85) | data formatting | bytes 1048576

commit v4 on v3

--- a/solution.py
+++ b/solution.py
@@ -15,7 +15,8 @@
 KB = 4096
 BIG = 60 * 2**20
 EXTRA = 16
-LAG = 2
+LAG = 3
+SPREAD_AT = 3
 MESH = pl.DeviceIdType.MESH
 ANY = pl.BlockSpec(memory_space=pl.ANY)
 
@@ -87,9 +88,20 @@
     return tuple(jnp.int32(x) for x in DIGITS)
 
 
-def place_kernel(picks_ref, q_ref, out_ref, slot_ref, count_ref):
+def place_kernel(picks_ref, raw_ref, out_ref, slot_ref, q_ref, count_ref):
     heads, blocks, picked = picks_ref.shape
     item = q_ref.shape[1] // blocks
+    both = heads * item
+    streams = both // 16
+    to = lax.broadcasted_iota(jnp.int32, (both, both), 0)
+    frm = lax.broadcasted_iota(jnp.int32, (both, both), 1)
+    picking = (frm == lax.rem(to, 16) * streams + lax.div(to, 16)).astype(jnp.bfloat16)
+    for b in range(blocks):
+        rows = jnp.dot(
+            picking, raw_ref[b * both : (b + 1) * both, :], preferred_element_type=jnp.float32
+        ).astype(jnp.bfloat16)
+        for h in range(heads):
+            q_ref[h, b * item : (b + 1) * item, :] = rows[h * item : (h + 1) * item, :]
     owners = out_ref.shape[0]
     out_ref[...] = jnp.zeros_like(out_ref)
 
@@ -114,31 +126,36 @@
         lax.fori_loop(0, blocks, one, 0)
 
 
-def place(picks, q):
-    heads, rows, feature = q.shape
+def place(picks, raw):
+    heads, blocks, picked = picks.shape
+    feature = raw.shape[1]
+    rows = raw.shape[0] // heads
     return pl.pallas_call(
         place_kernel,
         out_shape=(
             jax.ShapeDtypeStruct((32, heads, 128, feature), jnp.bfloat16),
             jax.ShapeDtypeStruct(picks.shape, jnp.int32),
+            jax.ShapeDtypeStruct((heads, rows, feature), jnp.bfloat16),
         ),
         in_specs=[SM, VM],
-        out_specs=(VM, SM),
+        out_specs=(VM, SM, VM),
         scratch_shapes=[pltpu.SMEM((heads, 32), jnp.int32)],
         compiler_params=pltpu.CompilerParams(vmem_limit_bytes=BIG),
-    )(picks, q)
+    )(picks, raw)
 
 
 def exchange_kernel(
-    out_ref, key_ref, value_ref, q_ref, kv_ref, ret, own_ref, lse_ref,
-    raw, keys, values, arrived, done, kvs, acc_ref, top_ref, sum_ref,
-    load_sem, send_sem, recv_sem, back_sem, home_sem, kv_send, kv_recv, fwd_send, fwd_recv,
+    out_ref, key_ref, value_ref, q_ref, new_key_ref, new_value_ref, ret, own_ref, lse_ref,
+    kv_ref, raw, keys, values, arrived, done, kvs, acc_ref, top_ref, sum_ref,
+    load_sem, send_sem, recv_sem, back_sem, home_sem, kv_send, kv_recv, fwd_send, fwd_recv, spread_send,
 ):
     owners, heads, slot_rows, feature = out_ref.shape
     me = lax.axis_index("seq")
     z, x, core = lax.div(me, 8), lax.rem(lax.div(me, 2), 4), lax.rem(me, 2)
     sibling = me + 1 - 2 * core
-    place = lax.rem(z, 2) * 4 + x
+    lower = lax.rem(z, 2)
+    place = lower * 4 + x
+    sent_until = (1 - core) * (8 - place) + core * (4 - x)
     group, step = 4, 1024
 
     loads = [
@@ -195,6 +212,17 @@
             device_id_type=MESH,
         )
 
+    def kv_spread(o):
+        other = lax.rem(x + o, 4)
+        return pltpu.make_async_remote_copy(
+            src_ref=kvs.at[9],
+            dst_ref=kvs.at[2 * (4 + other - x) + 1],
+            send_sem=spread_send.at[o],
+            recv_sem=kv_recv.at[4 + other - x],
+            device_id={"seq": z * 8 + other * 2 + 1},
+            device_id_type=MESH,
+        )
+
     def kv_beside():
         return pltpu.make_async_remote_copy(
             src_ref=kv_ref,
@@ -221,6 +249,18 @@
     picking = (col == 2 * lax.rem(row, feature) + lax.div(row, feature)).astype(jnp.bfloat16)
     placing = (row == 2 * lax.rem(col, feature) + lax.div(col, feature)).astype(jnp.bfloat16)
 
+    for j in range(new_key_ref.shape[0] // span):
+        cut = slice(j * feature, (j + 1) * feature)
+        block = new_key_ref[j * span : (j + 1) * span, :]
+        both = jnp.dot(picking, block, preferred_element_type=jnp.float32).astype(jnp.bfloat16)
+        for h in range(heads):
+            kv_ref[0, h, cut, :] = both[h * feature : (h + 1) * feature, :]
+        block = new_value_ref[j * span : (j + 1) * span, :]
+        both = lax.dot_general(block, placing, TN, preferred_element_type=jnp.float32)
+        both = both.astype(jnp.bfloat16)
+        for h in range(heads):
+            kv_ref[1, h, cut, :] = both[:, h * feature : (h + 1) * feature]
+
     pl.semaphore_wait(barrier, owners - 1)
 
     def start_out(i, digits):
@@ -242,7 +282,11 @@
         kv_copy(d).start()
         return 0
 
-    lax.fori_loop(1, 8 - place, start_kv, 0)
+    lax.fori_loop(1, sent_until, start_kv, 0)
+
+    @pl.when((1 - lower) * core == 1)
+    def _():
+        kv_copy(4).start()
 
     @pl.when(core == 0)
     def _():
@@ -275,8 +319,17 @@
 
     lax.fori_loop(0, KB // feature, sort_values, 0, unroll=4)
 
+    spreads = lower * core
+
     def tile(i, digits):
         first = i * group
+
+        @pl.when(spreads * lax.div(i + 8 - SPREAD_AT, 8) * lax.div(8 + SPREAD_AT - i, 8) == 1)
+        def _():
+            kv_copy(4).wait_recv()
+            for o in range(1, 4):
+                kv_spread(o).start()
+
         offsets = offsets_of(digits)
         for j, offset in enumerate(offsets):
             if j == 0:
@@ -324,7 +377,10 @@
     half = kv_ref.shape[2] // 2
 
     def pass_on(d, _):
-        kv_copy(d).wait_recv()
+        @pl.when(jnp.logical_or(d != 4, spreads == 0))
+        def _():
+            kv_copy(d).wait_recv()
+
         kv_forward(d, core).start()
         return 0
 
@@ -389,7 +445,16 @@
         kv_copy(d).wait_send()
         return 0
 
-    lax.fori_loop(1, 8 - place, finish_kv, 0)
+    lax.fori_loop(1, sent_until, finish_kv, 0)
+
+    @pl.when((1 - lower) * core == 1)
+    def _():
+        kv_copy(4).wait_send()
+
+    @pl.when(spreads == 1)
+    def _():
+        for o in range(1, 4):
+            kv_spread(o).wait_send()
 
     @pl.when(core == 0)
     def _():
@@ -466,9 +531,10 @@
     )(picks, slots, table, own, lse, ret)
 
 
-def exchange(outgoing, keys, values, q, kv):
+def exchange(outgoing, keys, values, q, new_keys, new_values):
     owners, heads, slot_rows, feature = outgoing.shape
     rows = q.shape[1]
+    kv_shape = (2, heads, new_keys.shape[0] // heads, feature)
     back = (owners, heads * slot_rows + EXTRA, feature)
     dma = pltpu.SemaphoreType.DMA
     return pl.pallas_call(
@@ -478,15 +544,16 @@
             jax.ShapeDtypeStruct((heads, rows, feature), jnp.float32),
             jax.ShapeDtypeStruct((heads, 8, rows), jnp.float32),
         ),
-        in_specs=[VM, ANY, ANY, VM, VM],
+        in_specs=[VM, ANY, ANY, VM, VM, VM],
         out_specs=(VM, VM, VM),
         scratch_shapes=[
+            pltpu.VMEM(kv_shape, jnp.bfloat16),
             pltpu.VMEM((2,) + keys.shape, jnp.bfloat16),
             pltpu.VMEM((heads, KB, feature), jnp.bfloat16),
             pltpu.VMEM((heads, feature, KB), jnp.bfloat16),
             pltpu.VMEM(outgoing.shape, jnp.bfloat16),
             pltpu.VMEM(back, jnp.bfloat16),
-            pltpu.VMEM((16,) + kv.shape, jnp.bfloat16),
+            pltpu.VMEM((16,) + kv_shape, jnp.bfloat16),
             pltpu.VMEM((heads, feature, rows), jnp.float32),
             pltpu.VMEM((heads, 8, rows), jnp.float32),
             pltpu.VMEM((heads, 8, rows), jnp.float32),
@@ -499,11 +566,12 @@
             dma((8,)),
             dma((8,)),
             dma((8,)),
+            dma((4,)),
         ],
         compiler_params=pltpu.CompilerParams(
             collective_id=0, has_side_effects=True, vmem_limit_bytes=BIG
         ),
-    )(outgoing, keys, values, q, kv)
+    )(outgoing, keys, values, q, new_keys, new_values)
 
 
 def project_kernel(
@@ -583,7 +651,7 @@
 def project(merged, weight):
     rows, depth = merged.shape
     width = weight.shape[1]
-    parts = 8
+    parts = 16
     wide = width // parts
     quarter = rows // 4
     dma = pltpu.SemaphoreType.DMA
@@ -614,13 +682,9 @@
 
 
 def on_device(queries, ctx_keys, ctx_values, new_keys, new_values, picks, out_weight):
-    q = queries.reshape(16, 16, 2, 4, 128).transpose(2, 0, 3, 1, 4).reshape(2, 1024, 128)
-    outgoing, slots = place(picks, q)
-    keys = ctx_keys.reshape(8192, 128)
-    values = ctx_values.reshape(8192, 128)
-    new_t = new_values.reshape(2, 128, 2, 128).transpose(2, 0, 3, 1).reshape(2, 256, 128)
-    kv = jnp.stack([new_keys.transpose(1, 0, 2), new_t])
-    ret, own, lse = exchange(outgoing, keys, values, q, kv)
+    outgoing, slots, q = place(picks, queries.reshape(2048, 128))
+    flat = [x.reshape(-1, 128) for x in (ctx_keys, ctx_values, new_keys, new_values)]
+    ret, own, lse = exchange(outgoing, flat[0], flat[1], q, flat[2], flat[3])
     merged = merge(picks, slots, own, lse, ret)
     return project(merged, out_weight)
 

time: 137 us -> 132 us (0.964)
  the two profiles are of different devices: /device:TPU:1 before, /device:TPU:40 now
where the time goes in v4:
time: 132 us; the launch traced here: 131 us
  Pallas kernels  128 us (97%)
  local copies, waits for them, and re-layouts  3.23 us (2%)
    pallas_call x1, Pallas kernels, exchange(): pl.pallas_call(exchange_kernel, out_shape=(jax.ShapeDtypeStruct(back, jnp...  90.2 us
    pallas_call x1, Pallas kernels, project(): pl.pallas_call(project_kernel, out_shape=jax.ShapeDtypeStruct((quarter, w...  28.7 us
    pallas_call x1, Pallas kernels, merge(): pl.pallas_call(merge_kernel, out_shape=jax.ShapeDtypeStruct((256, 8 * own...  5.44 us
    pallas_call x1, Pallas kernels, place(): pl.pallas_call(place_kernel, out_shape=(jax.ShapeDtypeStruct((32, heads,...  3.84 us
    unnamed x2, local copies, waits for them, and re-layouts  3.23 us

profile of v4, /device:TPU:40, one launch (start us, length us, event | category | flops | bytes accessed | tf_op | source)
XLA Modules:
  0.0 131.5 jit_solution(15616423748487670076)
XLA Ops:
  0.0 1.4 %copy.10.picks_ref = s32[2,16,2]{2,1,0:T(8,128)} copy(s32[2,16,2]{1,2,0:T(2,128)} %param.13) | data formatting | bytes 512 | tf_op args[5]
  1.4 3.8 %shard_map.82 = (bf16[32,2,128,128]{3,2,1,0:T(8,128)(2,1)}, s32[2,16,2]{2,1,0:T(8,128)}, bf16[2,1024,128]{2,1,0:T(8,128)(2,1)}) custom-call(s32[2,16,2]{2,1,0:T(8,128)} %copy.10.picks_ref, bf16[2048,128]{1,0:T(8,128)(2,1)} %bitcast.7), custom_call_target="tpu_custom_call" | custom-call | tf_op jit(solution)/shard_map/pallas_call | solution.py:133
  5.2 90.2 %shard_map.83 = (bf16[32,272,128]{2,1,0:T(8,128)(2,1)}, f32[2,1024,128]{2,1,0:T(8,128)}, f32[2,8,1024]{2,1,0:T(8,128)}) custom-call(bf16[32,2,128,128]{3,2,1,0:T(8,128)(2,1)} %get-tuple-element.12.out_ref, bf16[8192,128]{1,0:T(8,128)(2,1)} %bitcast.5, bf16[8192,128]{1,0:T(8,128)(2,1)} %bitcast.6, bf16[2,1024,128]{2,1,0:T(8,128)(2,1)} %get-tuple-element.13.q_ref, ...), custom_call_target="tpu_custom_call" | custom-call | tf_op jit(solution)/shard_map/pallas_call | solution.py:540
  95.4 5.4 %shard_map.84.m_ref = bf16[256,1024]{1,0:T(8,128)(2,1)} custom-call(s32[2,16,2]{2,1,0:T(8,128)} %copy.10.picks_ref, s32[2,16,2]{2,1,0:T(8,128)} %get-tuple-element.11.slot_ref, s32[4,4]{1,0:T(4,128)} %constant.2.clone.table_ref, f32[2,1024,128]{2,1,0:T(8,128)} %get-tuple-element.14.own_ref, f32[2,8,1024]{2,1,0:T(8,128)} %get-tuple-element.15.own_lse_ref, ...), custom_call_target="tpu_custom_call" | custom-call | tf_op jit(solution)/shard_map/pallas_call | solution.py:525
  100.8 28.7 %shard_map.85 = bf16[64,4096]{1,0:T(8,128)(2,1)} custom-call(bf16[256,1024]{1,0:T(8,128)(2,1)} %shard_map.84.m_ref, bf16[1024,4096]{1,0:T(8,128)(2,1)} %w_ref.1), custom_call_target="tpu_custom_call" | custom-call | tf_op jit(solution)/shard_map/pallas_call | solution.py:658
  129.6 1.9 %copy.12 = bf16[64,4096]{1,0:T(8,128)(2,1)} copy(bf16[64,4096]{1,0:T(8,128)(2,1)} %shard_map.85) | data formatting | bytes 1048576

commit v5 on v4

--- a/solution.py
+++ b/solution.py
@@ -16,7 +16,9 @@
 BIG = 60 * 2**20
 EXTRA = 16
 LAG = 3
-SPREAD_AT = 3
+EARLY = 2
+SPREAD_AT = 2
+OWN_AT = 5
 MESH = pl.DeviceIdType.MESH
 ANY = pl.BlockSpec(memory_space=pl.ANY)
 
@@ -276,7 +278,7 @@
                 outward(k, ahead(offset)).start()
         return next_digits(digits)
 
-    lax.fori_loop(0, owners // group, start_out, first_digits())
+    digits = lax.fori_loop(0, EARLY, start_out, first_digits())
 
     def start_kv(d, _):
         kv_copy(d).start()
@@ -292,6 +294,7 @@
     def _():
         kv_beside().start()
 
+    lax.fori_loop(EARLY, owners // group, start_out, digits)
     arrived[0] = out_ref[me]
     loads[0].wait()
 
@@ -321,14 +324,80 @@
 
     spreads = lower * core
 
+    def own_attention():
+        item = slot_rows // 2
+        block_rows = item // 4
+        half = kv_ref.shape[2] // 2
+
+        def pass_on(d, _):
+            @pl.when(jnp.logical_or(d != 4, spreads == 0))
+            def _():
+                kv_copy(d).wait_recv()
+
+            kv_forward(d, core).start()
+            return 0
+
+        lax.fori_loop(1, place + 1, pass_on, 0)
+
+        def absorb(pairs, first):
+            for h in range(heads):
+                split = split_queries(q_ref[h])
+                key_rows = [ref[0, h] for ref in pairs]
+                key_rows = key_rows[0] if len(pairs) == 1 else jnp.concatenate(key_rows, axis=0)
+                value_t = jnp.concatenate(
+                    [ref[1, h, at : at + half, :] for ref in pairs for at in (0, half)], axis=1
+                )
+                s = scores_of(key_rows, split)
+                if first:
+                    key_at = lax.broadcasted_iota(jnp.int32, s.shape, 0)
+                    lane = lax.broadcasted_iota(jnp.int32, s.shape, 1)
+                    row_at = (lane // item) * block_rows + lax.rem(lane, block_rows)
+                    s = jnp.where(key_at <= row_at, s, -1e30)
+                best = jnp.max(s, axis=0, keepdims=True)
+                if not first:
+                    best = jnp.maximum(top_ref[h, 0:1, :], best)
+                e = jnp.exp2(s - best)
+                part = jnp.sum(e, axis=0, keepdims=True)
+                o = jnp.dot(value_t, e.astype(jnp.bfloat16), preferred_element_type=jnp.float32)
+                if first:
+                    acc_ref[h] = o
+                    sum_ref[h, 0:1, :] = part
+                else:
+                    fade = jnp.exp2(top_ref[h, 0:1, :] - best)
+                    acc_ref[h] = acc_ref[h] * fade + o
+                    sum_ref[h, 0:1, :] = sum_ref[h, 0:1, :] * fade + part
+                top_ref[h, 0:1, :] = best
+
+        absorb([kv_ref], True)
+
+        @pl.when(core == 1)
+        def _():
+            kv_beside().wait_recv()
+            absorb([kvs.at[0]], False)
+
+        def two(d, _):
+            kv_forward(d, core).wait_recv()
+            absorb([kvs.at[2 * d], kvs.at[2 * d + 1]], False)
+            return 0
+
+        lax.fori_loop(1, place + 1, two, 0)
+        for h in range(heads):
+            total = sum_ref[h, 0:1, :]
+            own_ref[h] = (acc_ref[h] / total).T
+            lse_ref[h] = jnp.broadcast_to(top_ref[h, 0:1, :] + jnp.log2(total), lse_ref.shape[1:])
+
     def tile(i, digits):
         first = i * group
 
-        @pl.when(spreads * lax.div(i + 8 - SPREAD_AT, 8) * lax.div(8 + SPREAD_AT - i, 8) == 1)
+        @pl.when(jnp.logical_and(i == SPREAD_AT, spreads == 1))
         def _():
             kv_copy(4).wait_recv()
             for o in range(1, 4):
                 kv_spread(o).start()
+
+        @pl.when(i == OWN_AT)
+        def _():
+            own_attention()
 
         offsets = offsets_of(digits)
         for j, offset in enumerate(offsets):
@@ -371,67 +440,6 @@
 
     lax.fori_loop(0, owners // group, tile, first_digits())
     ret[0] = done[0]
-
-    item = slot_rows // 2
-    block_rows = item // 4
-    half = kv_ref.shape[2] // 2
-
-    def pass_on(d, _):
-        @pl.when(jnp.logical_or(d != 4, spreads == 0))
-        def _():
-            kv_copy(d).wait_recv()
-
-        kv_forward(d, core).start()
-        return 0
-
-    lax.fori_loop(1, place + 1, pass_on, 0)
-
-    def absorb(pairs, first):
-        for h in range(heads):
-            split = split_queries(q_ref[h])
-            key_rows = [ref[0, h] for ref in pairs]
-            key_rows = key_rows[0] if len(pairs) == 1 else jnp.concatenate(key_rows, axis=0)
-            value_t = jnp.concatenate(
-                [ref[1, h, at : at + half, :] for ref in pairs for at in (0, half)], axis=1
-            )
-            s = scores_of(key_rows, split)
-            if first:
-                key_at = lax.broadcasted_iota(jnp.int32, s.shape, 0)
-                lane = lax.broadcasted_iota(jnp.int32, s.shape, 1)
-                row_at = (lane // item) * block_rows + lax.rem(lane, block_rows)
-                s = jnp.where(key_at <= row_at, s, -1e30)
-            best = jnp.max(s, axis=0, keepdims=True)
-            if not first:
-                best = jnp.maximum(top_ref[h, 0:1, :], best)
-            e = jnp.exp2(s - best)
-            part = jnp.sum(e, axis=0, keepdims=True)
-            o = jnp.dot(value_t, e.astype(jnp.bfloat16), preferred_element_type=jnp.float32)
-            if first:
-                acc_ref[h] = o
-                sum_ref[h, 0:1, :] = part
-            else:
-                fade = jnp.exp2(top_ref[h, 0:1, :] - best)
-                acc_ref[h] = acc_ref[h] * fade + o
-                sum_ref[h, 0:1, :] = sum_ref[h, 0:1, :] * fade + part
-            top_ref[h, 0:1, :] = best
-
-    absorb([kv_ref], True)
-
-    @pl.when(core == 1)
-    def _():
-        kv_beside().wait_recv()
-        absorb([kvs.at[0]], False)
-
-    def two(d, _):
-        kv_forward(d, core).wait_recv()
-        absorb([kvs.at[2 * d], kvs.at[2 * d + 1]], False)
-        return 0
-
-    lax.fori_loop(1, place + 1, two, 0)
-    for h in range(heads):
-        total = sum_ref[h, 0:1, :]
-        own_ref[h] = (acc_ref[h] / total).T
-        lse_ref[h] = jnp.broadcast_to(top_ref[h, 0:1, :] + jnp.log2(total), lse_ref.shape[1:])
 
     def finish(k, _):
         homeward(k, sibling).wait_recv()

time: 132 us -> 145 us (1.098)
  Pallas kernels: 128 us -> 142 us
    pallas_call x1, Pallas kernels: 90.2 us -> 104 us  [exchange(): pl.pallas_call(exchange_kernel, out_shape=(jax.ShapeDtypeStruct(back, jnp...]
where the time goes in v5:
time: 145 us
  Pallas kernels  142 us (98%)
  local copies, waits for them, and re-layouts  3.23 us (2%)
    pallas_call x1, Pallas kernels, exchange(): pl.pallas_call(exchange_kernel, out_shape=(jax.ShapeDtypeStruct(back, jnp...  104 us
    pallas_call x1, Pallas kernels, project(): pl.pallas_call(project_kernel, out_shape=jax.ShapeDtypeStruct((quarter, w...  28.7 us
    pallas_call x1, Pallas kernels, merge(): pl.pallas_call(merge_kernel, out_shape=jax.ShapeDtypeStruct((256, 8 * own...  5.44 us
    pallas_call x1, Pallas kernels, place(): pl.pallas_call(place_kernel, out_shape=(jax.ShapeDtypeStruct((32, heads,...  3.84 us
    unnamed x2, local copies, waits for them, and re-layouts  3.23 us

profile of v5, /device:TPU:40, one launch (start us, length us, event | category | flops | bytes accessed | tf_op | source)
XLA Modules:
  0.0 145.0 jit_solution(12944060458828079243)
XLA Ops:
  0.0 1.4 copy.10.picks_ref
  1.4 3.8 %shard_map.82 = (bf16[32,2,128,128]{3,2,1,0:T(8,128)(2,1)}, s32[2,16,2]{2,1,0:T(8,128)}, bf16[2,1024,128]{2,1,0:T(8,128)(2,1)}) custom-call(s32[2,16,2]{2,1,0:T(8,128)} %copy.10.picks_ref, bf16[2048,128]{1,0:T(8,128)(2,1)} %bitcast.7), custom_call_target="tpu_custom_call" | custom-call | tf_op jit(solution)/shard_map/pallas_call | solution.py:135
  5.2 103.7 %shard_map.83 = (bf16[32,272,128]{2,1,0:T(8,128)(2,1)}, f32[2,1024,128]{2,1,0:T(8,128)}, f32[2,8,1024]{2,1,0:T(8,128)}) custom-call(bf16[32,2,128,128]{3,2,1,0:T(8,128)(2,1)} %get-tuple-element.12.out_ref, bf16[8192,128]{1,0:T(8,128)(2,1)} %bitcast.5, bf16[8192,128]{1,0:T(8,128)(2,1)} %bitcast.6, bf16[2,1024,128]{2,1,0:T(8,128)(2,1)} %get-tuple-element.13.q_ref, ...), custom_call_target="tpu_custom_call" | custom-call | tf_op jit(solution)/shard_map/pallas_call | solution.py:548
  109.0 5.4 %shard_map.84.m_ref = bf16[256,1024]{1,0:T(8,128)(2,1)} custom-call(s32[2,16,2]{2,1,0:T(8,128)} %copy.10.picks_ref, s32[2,16,2]{2,1,0:T(8,128)} %get-tuple-element.11.slot_ref, s32[4,4]{1,0:T(4,128)} %constant.2.clone.table_ref, f32[2,1024,128]{2,1,0:T(8,128)} %get-tuple-element.14.own_ref, f32[2,8,1024]{2,1,0:T(8,128)} %get-tuple-element.15.own_lse_ref, ...), custom_call_target="tpu_custom_call" | custom-call | tf_op jit(solution)/shard_map/pallas_call | solution.py:533
  114.4 28.7 %shard_map.85 = bf16[64,4096]{1,0:T(8,128)(2,1)} custom-call(bf16[256,1024]{1,0:T(8,128)(2,1)} %shard_map.84.m_ref, bf16[1024,4096]{1,0:T(8,128)(2,1)} %w_ref.1), custom_call_target="tpu_custom_call" | custom-call | tf_op jit(solution)/shard_map/pallas_call | solution.py:666
  143.1 1.9 %copy.12 = bf16[64,4096]{1,0:T(8,128)(2,1)} copy(bf16[64,4096]{1,0:T(8,128)(2,1)} %shard_map.85) | data formatting | bytes 1048576

commit v6 on v5

--- a/solution.py
+++ b/solution.py
@@ -16,9 +16,8 @@
 BIG = 60 * 2**20
 EXTRA = 16
 LAG = 3
-EARLY = 2
-SPREAD_AT = 2
-OWN_AT = 5
+EARLY = 4
+SPREAD_AT = 5
 MESH = pl.DeviceIdType.MESH
 ANY = pl.BlockSpec(memory_space=pl.ANY)
 
@@ -395,10 +394,6 @@
             for o in range(1, 4):
                 kv_spread(o).start()
 
-        @pl.when(i == OWN_AT)
-        def _():
-            own_attention()
-
         offsets = offsets_of(digits)
         for j, offset in enumerate(offsets):
             if j == 0:
@@ -439,6 +434,7 @@
         return next_digits(digits)
 
     lax.fori_loop(0, owners // group, tile, first_digits())
+    own_attention()
     ret[0] = done[0]
 
     def finish(k, _):

time: 145 us -> 126 us (0.87)
  the two profiles are of different devices: /device:TPU:40 before, /device:TPU:45 now
where the time goes in v6:
time: 126 us
  Pallas kernels  123 us (98%)
  local copies, waits for them, and re-layouts  3.23 us (3%)
    pallas_call x1, Pallas kernels, exchange(): pl.pallas_call(exchange_kernel, out_shape=(jax.ShapeDtypeStruct(back, jnp...  88 us
    pallas_call x1, Pallas kernels, project(): pl.pallas_call(project_kernel, out_shape=jax.ShapeDtypeStruct((quarter, w...  25.3 us
    pallas_call x1, Pallas kernels, merge(): pl.pallas_call(merge_kernel, out_shape=jax.ShapeDtypeStruct((256, 8 * own...  5.43 us
    pallas_call x1, Pallas kernels, place(): pl.pallas_call(place_kernel, out_shape=(jax.ShapeDtypeStruct((32, heads,...  3.84 us
    unnamed x2, local copies, waits for them, and re-layouts  3.23 us

profile of v6, /device:TPU:45, one launch (start us, length us, event | category | flops | bytes accessed | tf_op | source)
XLA Modules:
  0.0 125.8 jit_solution(9534118116208883488)
XLA Ops:
  0.0 1.4 %copy.10.picks_ref = s32[2,16,2]{2,1,0:T(8,128)} copy(s32[2,16,2]{1,2,0:T(2,128)} %param.13) | data formatting | bytes 512 | tf_op args[5]
  1.4 3.8 %shard_map.82 = (bf16[32,2,128,128]{3,2,1,0:T(8,128)(2,1)}, s32[2,16,2]{2,1,0:T(8,128)}, bf16[2,1024,128]{2,1,0:T(8,128)(2,1)}) custom-call(s32[2,16,2]{2,1,0:T(8,128)} %copy.10.picks_ref, bf16[2048,128]{1,0:T(8,128)(2,1)} %bitcast.7), custom_call_target="tpu_custom_call" | custom-call | tf_op jit(solution)/shard_map/pallas_call | solution.py:134
  5.2 88.0 %shard_map.83 = (bf16[32,272,128]{2,1,0:T(8,128)(2,1)}, f32[2,1024,128]{2,1,0:T(8,128)}, f32[2,8,1024]{2,1,0:T(8,128)}) custom-call(bf16[32,2,128,128]{3,2,1,0:T(8,128)(2,1)} %get-tuple-element.12.out_ref, bf16[8192,128]{1,0:T(8,128)(2,1)} %bitcast.5, bf16[8192,128]{1,0:T(8,128)(2,1)} %bitcast.6, bf16[2,1024,128]{2,1,0:T(8,128)(2,1)} %get-tuple-element.13.q_ref, ...), custom_call_target="tpu_custom_call" | custom-call | tf_op jit(solution)/shard_map/pallas_call | solution.py:544
  93.2 5.4 %shard_map.84.m_ref = bf16[256,1024]{1,0:T(8,128)(2,1)} custom-call(s32[2,16,2]{2,1,0:T(8,128)} %copy.10.picks_ref, s32[2,16,2]{2,1,0:T(8,128)} %get-tuple-element.11.slot_ref, s32[4,4]{1,0:T(4,128)} %constant.2.clone.table_ref, f32[2,1024,128]{2,1,0:T(8,128)} %get-tuple-element.14.own_ref, f32[2,8,1024]{2,1,0:T(8,128)} %get-tuple-element.15.own_lse_ref, ...), custom_call_target="tpu_custom_call" | custom-call | tf_op jit(solution)/shard_map/pallas_call | solution.py:529
  98.6 25.3 %shard_map.85 = bf16[64,4096]{1,0:T(8,128)(2,1)} custom-call(bf16[256,1024]{1,0:T(8,128)(2,1)} %shard_map.84.m_ref, bf16[1024,4096]{1,0:T(8,128)(2,1)} %w_ref.1), custom_call_target="tpu_custom_call" | custom-call | tf_op jit(solution)/shard_map/pallas_call | solution.py:662
  124.0 1.9 %copy.12 = bf16[64,4096]{1,0:T(8,128)(2,1)} copy(bf16[64,4096]{1,0:T(8,128)(2,1)} %shard_map.85) | data formatting | bytes 1048576
